TPU v7x, 32 devices: a whole 2x2x4 slice. The times are simulated.
32 devices in a mesh: ctx: 16 (over z, y, core), head: 2 (over x).
Axes of the slice: x: 2, y: 2, z: 4, core: 2. Of those that a mesh axis runs over, the one named last changes fastest.
Arguments:
- prompt_latent: bfloat16 [1536, 576], P('ctx'), may hold values from -8 to 8
- prefill_query: bfloat16 [1024, 64, 192], P('ctx', 'head'), may hold values from -12 to 12
- span_start: int32 [1], replicated, may hold values from 0 to 512
- w_uk: bfloat16 [64, 128, 512], P('head'), may hold values from -0.5 to 0.5
- w_uv: bfloat16 [64, 512, 128], P('head'), may hold values from -0.25 to 0.25
- decode_latent: bfloat16 [64, 64, 576], P(None, 'ctx'), may hold values from -8 to 8
- owner_slot: int32 [64], replicated, may hold values from 0 to 63, each once
- lengths: int32 [64], P('ctx'), may hold values from 1 to 64
- hidden_new: bfloat16 [4, 64, 7168], P(None, 'ctx', 'head'), may hold values from -6 to 6
- decode_query: bfloat16 [4, 64, 64, 192], P(None, 'ctx', 'head'), may hold values from -12 to 12
- w_down: bfloat16 [7168, 576], P('head'), may hold values from -0.0625 to 0.0625
- kv_gain: float32 [512], replicated, may hold values from 0.5 to 1.5
Outputs:
- prefill_out: bfloat16 [1024, 64, 128], P('ctx', 'head')
- decode_out: bfloat16 [4, 64, 64, 128], P(None, 'ctx', 'head')
Inputs may be any that keep to these rules, and one draw needn't show every extreme that they name: span_start + 1024 <= 1536. `owner_slot`: each slot once.
All inputs are finite; a program needn't handle non-finite values.
Results may differ from a plain program's by a relative error of at most 0.014.
Values may be sent and summed in bfloat16 or wider, within the bound.
A program may use at most 128 MiB of HBM per device.

v0:
```python
import jax
import jax.numpy as jnp
from jax import lax
from jax.sharding import PartitionSpec as P

KV_RANK = 512
ROPE = 64
NOPE = 128


def absorb(query, w_uk, form):
    absorbed = jnp.einsum(form, query[..., :NOPE], w_uk, preferred_element_type=jnp.float32).astype(
        jnp.bfloat16
    )
    return jnp.concatenate([absorbed, query[..., NOPE:]], axis=-1)


def body(
    prompt_latent,
    prefill_query,
    span_start,
    w_uk,
    w_uv,
    decode_latent,
    owner_slot,
    lengths,
    hidden_new,
    decode_query,
    w_down,
    kv_gain,
):
    scale = (NOPE + ROPE) ** (-0.5)
    heads_here = w_uk.shape[0]
    queries = prefill_query.shape[0]
    width = prompt_latent.shape[1]
    full_query = absorb(prefill_query, w_uk, "qhn,hnc->qhc")
    rows = full_query.reshape(queries * heads_here, width)
    first = span_start[0] + lax.axis_index("ctx") * queries
    positions = jnp.repeat(first + jnp.arange(queries, dtype=jnp.int32), heads_here)
    count = rows.shape[0]
    piece = lax.all_gather(prompt_latent, "ctx", axis=0, tiled=True)
    top = jnp.full((count,), -1e30, jnp.float32)
    scores = jnp.dot(rows, piece.T, preferred_element_type=jnp.float32) * scale
    keys = jnp.arange(piece.shape[0], dtype=jnp.int32)
    allowed = keys[None, :] <= positions[:, None]
    peak = jnp.maximum(top, jnp.max(jnp.where(allowed, scores, -1e30), axis=1))
    probs = jnp.where(allowed, jnp.exp(scores - peak[:, None]), 0.0)
    total = jnp.sum(probs, axis=1)
    acc = jnp.dot(
        probs.astype(jnp.bfloat16), piece[:, :KV_RANK], preferred_element_type=jnp.float32
    )
    top, total, acc = (peak, total, acc)
    mixed = (acc / total[:, None]).astype(jnp.bfloat16).reshape(queries, heads_here, KV_RANK)
    prefill_out = jnp.einsum(
        "qhc,hcv->qhv", mixed, w_uv, preferred_element_type=jnp.float32
    ).astype(jnp.bfloat16)
    order = jnp.argsort(owner_slot)
    by_slot = decode_latent[order]
    cache = lax.all_to_all(by_slot, "ctx", split_axis=0, concat_axis=1, tiled=True)
    steps_here, owned, model_cols = hidden_new.shape
    raw_part = jnp.dot(
        hidden_new.reshape(steps_here * owned, model_cols),
        w_down,
        preferred_element_type=jnp.float32,
    )
    raw = lax.psum(raw_part.astype(jnp.bfloat16), "head").astype(jnp.float32)
    front = raw[:, :KV_RANK]
    factor = lax.rsqrt(jnp.mean(front * front, axis=1) + 1e-06)
    normed = front * factor[:, None] * kv_gain[None, :]
    new_rows = jnp.concatenate([normed, raw[:, KV_RANK:]], axis=1).astype(jnp.bfloat16)
    new_latent = new_rows.reshape(steps_here, owned, width)
    query = absorb(decode_query, w_uk, "srhn,hnc->srhc")
    cache_scores = (
        jnp.einsum("srhc,rjc->srhj", query, cache, preferred_element_type=jnp.float32) * scale
    )
    new_scores = (
        jnp.einsum("srhc,trc->srht", query, new_latent, preferred_element_type=jnp.float32) * scale
    )
    capacity = cache.shape[1]
    cache_ok = (jnp.arange(capacity, dtype=jnp.int32)[None, :] < lengths[:, None])[None, :, None, :]
    steps_idx = jnp.arange(steps_here, dtype=jnp.int32)
    new_ok = (steps_idx[None, :] <= steps_idx[:, None])[:, None, None, :]
    peak = jnp.maximum(
        jnp.max(jnp.where(cache_ok, cache_scores, -1e30), axis=3),
        jnp.max(jnp.where(new_ok, new_scores, -1e30), axis=3),
    )
    cache_p = jnp.where(cache_ok, jnp.exp(cache_scores - peak[..., None]), 0.0)
    new_p = jnp.where(new_ok, jnp.exp(new_scores - peak[..., None]), 0.0)
    total_d = jnp.sum(cache_p, axis=3) + jnp.sum(new_p, axis=3)
    mixed_d = jnp.einsum(
        "srhj,rjc->srhc",
        cache_p.astype(jnp.bfloat16),
        cache[:, :, :KV_RANK],
        preferred_element_type=jnp.float32,
    )
    mixed_d = mixed_d + jnp.einsum(
        "srht,trc->srhc",
        new_p.astype(jnp.bfloat16),
        new_latent[:, :, :KV_RANK],
        preferred_element_type=jnp.float32,
    )
    mixed_d = (mixed_d / total_d[..., None]).astype(jnp.bfloat16)
    decode_out = jnp.einsum(
        "srhc,hcv->srhv", mixed_d, w_uv, preferred_element_type=jnp.float32
    ).astype(jnp.bfloat16)
    return (prefill_out, decode_out)


def solution(mesh):
    in_specs = (
        P("ctx", None),
        P("ctx", "head", None),
        P(),
        P("head", None, None),
        P("head", None, None),
        P(None, "ctx", None),
        P(),
        P("ctx"),
        P(None, "ctx", "head"),
        P(None, "ctx", "head", None),
        P("head", None),
        P(),
    )
    out_specs = (P("ctx", "head", None), P(None, "ctx", "head", None))
    return jax.shard_map(body, mesh=mesh, in_specs=in_specs, out_specs=out_specs, check_vma=False)
```

profile of v0, /device:TPU:0, one launch (start us, length us, event | category | flops | bytes accessed | tf_op | source)
XLA Modules:
  0.0 81.2 jit_solution(5941769488176060839)
XLA Ops:
  7.2 0.7 all-gather.2.cloned.1.call-update
  7.9 2.7 %sort.17 = (s32[64]{0:T(128)}, s32[64]{0:T(128)S(1)}) sort(s32[64]{0:T(128)} %param.18, s32[64]{0:T(128)S(1)} %iota.33), dimensions={0}, to_apply=%region_2.3 | sort | flops 384 | bytes 1024 | tf_op jit(solution)/shard_map/jit(argsort)/sort | solution.py:57
  10.7 1.6 %gather_fusion = bf16[64,4,576]{2,1,0:T(4,128)(2,1)} fusion(bf16[64,4,576]{2,1,0:T(4,128)(2,1)S(1)} %copy-done, s32[1024]{0:T(1024)S(1)} %pad_clamp_fusion), kind=kCustom, calls=%fused_computation | custom fusion | bytes 590080 | tf_op jit(solution)/shard_map/gather | solution.py:58
  12.2 7.4 %all-to-all-start = ((bf16[64,4,576]{2,1,0:T(4,128)(2,1)}), bf16[64,4,576]{2,1,0:T(4,128)(2,1)}, u32[]{:S(2)}, u32[]{:S(2)}) async-start(bf16[64,4,576]{2,1,0:T(4,128)(2,1)} %gather_fusion), calls=%async_computation | async-start | bytes 655360 | tf_op jit(solution)/shard_map/all_to_all | solution.py:59
  20.7 2.9 %convert_bitcast_fusion = bf16[64,32,512]{2,0,1:T(8,128)(2,1)S(1)} fusion(bf16[32,128,512]{2,1,0:T(8,128)(2,1)} %param.15, bf16[64,32,128]{2,1,0:T(8,128)(2,1)S(1)} %slice-done.1), kind=kOutput, calls=%fused_computation.15 | convolution fusion | flops 269484032 | bytes 6815744 | tf_op jit(solution)/shard_map/qhn,hnc->qhc/dot_general | solution.py:12
  24.1 1.5 %copy.41 = bf16[64,32,576]{2,1,0:T(8,128)(2,1)S(1)} copy(bf16[64,32,576]{2,0,1:T(8,128)(2,1)S(1)} %pad_maximum_fusion) | data formatting | bytes 4718592 | tf_op jit(solution)/shard_map/concatenate | solution.py:15
  25.7 3.3 %convolution_convert_fusion = bf16[16,576]{1,0:T(8,128)(2,1)S(1)} fusion(bf16[16,3584]{1,0:T(8,128)(2,1)S(1)} %reshape.70, bf16[3584,576]{0,1:T(8,128)(2,1)} %param.22), kind=kOutput, calls=%fused_computation.31 | convolution fusion | flops 66069504 | bytes 4261888 | tf_op jit(solution)/shard_map/dot_general | solution.py:61
  29.0 8.3 %psum.7 = bf16[16,576]{1,0:T(8,128)(2,1)S(1)} all-reduce(bf16[16,576]{1,0:T(8,128)(2,1)S(1)} %convolution_convert_fusion), channel_id=1, replica_groups=mesh['ctx'=16,'head'=2] {'head'}, use_global_device_ids=true, to_apply=%region_4.5 | all-reduce | flops 9216 | bytes 36864 | tf_op jit(solution)/shard_map/psum | solution.py:66
  37.6 2.9 %fusion.22 = bf16[4,4,32,512]{3,1,0,2:T(4,128)(2,1)S(1)} fusion(bf16[32,128,512]{2,1,0:T(8,128)(2,1)} %param.15, bf16[4,4,32,128]{3,2,1,0:T(8,128)(2,1)S(1)} %slice-done.3), kind=kOutput, calls=%fused_computation.23 | convolution fusion | flops 67371008 | bytes 4849664 | tf_op jit(solution)/shard_map/srhn,hnc->srhc/dot_general | solution.py:12
  41.0 0.7 copy-done.3
  41.7 0.6 select_reduce_fusion.2
  42.4 1.1 %copy.89 = bf16[16,4,4,576]{3,2,0,1:T(4,128)(2,1)S(1)} copy(bf16[16,4,4,576]{3,2,1,0:T(4,128)(2,1)} %bitcast.5) | data formatting | bytes 589824 | tf_op jit(solution)/shard_map/all_to_all | solution.py:59
  43.4 0.9 %all_to_all.16 = bf16[4,64,576]{2,1,0:T(8,128)(2,1)} reshape(bf16[4,16,4,576]{3,2,1,0:T(4,128)(2,1)S(1)} %bitcast.69) | data formatting | bytes 589824 | tf_op jit(solution)/shard_map/all_to_all | solution.py:59
  44.3 0.9 %reshape.81 = bf16[4,64,576,1]{2,1,0,3:T(8,128)(2,1)} reshape(bf16[4,16,4,576]{3,2,1,0:T(4,128)(2,1)S(1)} %bitcast.70) | data formatting | bytes 589824 | tf_op jit(solution)/shard_map/all_to_all | solution.py:59
  45.2 1.8 %select_reduce_fusion.1 = (f32[4,4,32]{2,0,1:T(4,128)S(1)}, f32[4,4,32,64]{3,2,0,1:T(8,128)S(1)}) fusion(pred[4,64]{1,0:T(4,128)(4,1)S(1)} %iota_compare_fusion.2, bf16[4,4,32,576]{3,1,0,2:T(4,128)(2,1)} %copy-done.3, bf16[4,64,576,1]{2,1,0,3:T(8,128)(2,1)} %reshape.81), kind=kOutput, calls=%fused_computation.42 | convolution fusion | flops 37846528 | bytes 1018112 | tf_op jit(solution)/shard_map/srhc,rjc->srhj/dot_general | solution.py:74
  47.4 1.3 %fusion.41 = f32[4,512,4,32]{1,3,2,0:T(8,128)S(1)} fusion(bf16[4,64,576]{2,1,0:T(8,128)(2,1)} %all_to_all.16, f32[4,4,32,64]{3,2,0,1:T(8,128)S(1)} %get-tuple-element.13, f32[4,4,32]{2,0,1:T(4,128)S(1)} %max.7, pred[4,64]{1,0:T(4,128)(4,1)S(1)} %iota_compare_fusion.2), kind=kOutput, calls=%fused_computation.40 | convolution fusion | flops 33652736 | bytes 1444096 | tf_op jit(solution)/shard_map/srhj,rjc->srhc/dot_general | solution.py:90
  49.1 0.9 %fusion.32 = bf16[4,4,32,128]{3,1,0,2:T(4,128)(2,1)S(1)} fusion(bf16[32,512,128]{2,1,0:T(8,128)(2,1)S(1)} %copy-done.1, bf16[4,4,32,512]{3,2,0,1:T(8,128)(2,1)S(1)} %fusion.21), kind=kOutput, calls=%fused_computation.28 | convolution fusion | flops 67174400 | bytes 4849664 | tf_op jit(solution)/shard_map/srhc,hcv->srhv/dot_general | solution.py:103
  50.0 0.7 copy.53
  50.7 5.4 %all-gather.2.cloned.1.call-done = bf16[1536,576]{1,0:T(8,128)(2,1)} async-done(((bf16[96,576]{1,0:T(8,128)(2,1)}), bf16[1536,576]{1,0:T(8,128)(2,1)}) %all-gather.2.cloned.1.call-update) | async-done | bytes 1769488 | tf_op jit(solution)/shard_map/all_gather | solution.py:41
  56.1 7.2 %select_reduce_fusion = (f32[2048]{0:T(1024)S(1)}, f32[2048,1536]{0,1:T(8,128)S(1)}) fusion(s32[2048]{0:T(1024)S(1)} %le.39, bf16[2048,576]{1,0:T(8,128)(2,1)S(1)} %bitcast.71, bf16[1536,576]{1,0:T(8,128)(2,1)} %all-gather.2.cloned.1.call-done), kind=kOutput, calls=%fused_computation.2 | convolution fusion | flops 3636459520 | bytes 16728064 | tf_op jit(solution)/shard_map/dot_general | solution.py:43
  63.3 3.5 %fusion = f32[2048]{0:T(1024)S(1)} fusion(f32[2048,1536]{0,1:T(8,128)S(1)} %get-tuple-element.11, f32[2048]{0:T(1024)S(1)} %broadcast_maximum_fusion, s32[2048]{0:T(1024)S(1)} %le.39), kind=kLoop, calls=%fused_computation.4 | loop fusion | flops 15726592 | bytes 12607488 | tf_op jit(solution)/shard_map/reduce_sum | solution.py:48
  66.9 3.8 %divide_convert_fusion = bf16[2048,512]{1,0:T(8,128)(2,1)S(1)} fusion(f32[2048]{0:T(1024)S(1)} %fusion, f32[2048,1536]{0,1:T(8,128)S(1)} %get-tuple-element.11, f32[2048]{0:T(1024)S(1)} %broadcast_maximum_fusion, s32[2048]{0:T(1024)S(1)} %le.39, bf16[1536,576]{1,0:T(8,128)(2,1)S(1)} %copy-done.6), kind=kOutput, calls=%fused_computation.11 | convolution fusion | flops 3239051264 | bytes 16277504 | tf_op jit(solution)/shard_map/dot_general | solution.py:49
  70.7 2.5 %fusion.25 = bf16[64,32,128]{2,0,1:T(8,128)(2,1)S(1)} fusion(bf16[32,512,128]{2,1,0:T(8,128)(2,1)S(1)} %copy-done.2, bf16[64,32,512]{2,1,0:T(8,128)(2,1)S(1)} %bitcast.72), kind=kOutput, calls=%fused_computation.24 | convolution fusion | flops 268697600 | bytes 6815744 | tf_op jit(solution)/shard_map/qhc,hcv->qhv/dot_general | solution.py:54
  73.2 1.1 %copy.52 = bf16[64,32,128]{2,1,0:T(8,128)(2,1)} copy(bf16[64,32,128]{2,0,1:T(8,128)(2,1)S(1)} %fusion.25) | data formatting | bytes 1048576
  (51 shorter events, 2.4 us)
Async XLA Ops:
  7.2 3.5 %copy-start = (bf16[64,4,576]{2,1,0:T(4,128)(2,1)S(1)}, bf16[64,4,576]{2,1,0:T(4,128)(2,1)}, u32[]{:S(2)}) copy-start(bf16[64,4,576]{2,1,0:T(4,128)(2,1)} %param.17) | copy-start | bytes 884740
  7.2 13.3 %slice-start = ((bf16[64,32,192]{2,1,0:T(8,128)(2,1)}), bf16[64,32,64]{2,1,0:T(8,128)(2,1)S(1)}, s32[]{:S(2)}) async-start(bf16[64,32,192]{2,1,0:T(8,128)(2,1)} %param.13), calls=%async_computation.2 | async-start | bytes 1048576 | tf_op jit(solution)/shard_map/slice | solution.py:15
  7.2 13.5 %slice-start.1 = ((bf16[64,32,192]{2,1,0:T(8,128)(2,1)}), bf16[64,32,128]{2,1,0:T(8,128)(2,1)S(1)}, s32[]{:S(2)}) async-start(bf16[64,32,192]{2,1,0:T(8,128)(2,1)} %param.13), calls=%async_computation.3 | async-start | bytes 1048576 | tf_op jit(solution)/shard_map/slice | solution.py:12
  7.2 48.9 %all-gather.2.cloned.1.call-start = ((), (), s32[]{:S(2)}) async-start(), calls=%async_computation.1 | async-start | bytes 2088960 | tf_op jit(solution)/shard_map/all_gather | solution.py:41
  12.2 30.1 %all-to-all-start = ((bf16[64,4,576]{2,1,0:T(4,128)(2,1)}), bf16[64,4,576]{2,1,0:T(4,128)(2,1)}, u32[]{:S(2)}, u32[]{:S(2)}) async-start(bf16[64,4,576]{2,1,0:T(4,128)(2,1)} %gather_fusion), calls=%async_computation | async-start | bytes 655360 | tf_op jit(solution)/shard_map/all_to_all | solution.py:59
  23.6 1.9 %slice-start.2 = ((bf16[4,4,32,192]{3,2,1,0:T(8,128)(2,1)}), bf16[4,4,32,64]{3,2,1,0:T(8,128)(2,1)S(1)}, s32[]{:S(2)}) async-start(bf16[4,4,32,192]{3,2,1,0:T(8,128)(2,1)} %param.21), calls=%async_computation.4 | async-start | bytes 262144 | tf_op jit(solution)/shard_map/slice | solution.py:15
  23.7 2.0 %copy-start.4 = (bf16[4,4,3584]{2,1,0:T(4,128)(2,1)S(1)}, bf16[4,4,3584]{2,1,0:T(4,128)(2,1)}, u32[]{:S(2)}) copy-start(bf16[4,4,3584]{2,1,0:T(4,128)(2,1)} %param.20) | copy-start | bytes 344068
  24.0 13.5 %copy-start.5 = (f32[512]{0:T(512)S(1)}, f32[512]{0:T(512)}, u32[]{:S(2)}) copy-start(f32[512]{0:T(512)} %param.23) | copy-start | bytes 6148
  24.1 13.6 %slice-start.3 = ((bf16[4,4,32,192]{3,2,1,0:T(8,128)(2,1)}), bf16[4,4,32,128]{3,2,1,0:T(8,128)(2,1)S(1)}, s32[]{:S(2)}) async-start(bf16[4,4,32,192]{3,2,1,0:T(8,128)(2,1)} %param.21), calls=%async_computation.5 | async-start | bytes 262144 | tf_op jit(solution)/shard_map/slice | solution.py:12
  37.6 3.3 %copy-start.7 = (s32[4]{0:T(128)S(1)}, s32[4]{0:T(128)}, u32[]{:S(2)}) copy-start(s32[4]{0:T(128)} %param.19) | copy-start | bytes 52
  40.9 0.8 %copy-start.3 = (bf16[4,4,32,576]{3,1,0,2:T(4,128)(2,1)}, bf16[4,4,32,576]{3,1,0,2:T(4,128)(2,1)S(1)}, u32[]{:S(2)}) copy-start(bf16[4,4,32,576]{3,1,0,2:T(4,128)(2,1)S(1)} %pad_maximum_fusion.1) | copy-start | bytes 1769476
  45.2 3.9 %copy-start.1 = (bf16[32,512,128]{2,1,0:T(8,128)(2,1)S(1)}, bf16[32,512,128]{2,1,0:T(8,128)(2,1)}, u32[]{:S(2)}) copy-start(bf16[32,512,128]{2,1,0:T(8,128)(2,1)} %param.16) | copy-start | bytes 12582916
  63.3 3.5 %copy-start.6 = (bf16[1536,576]{1,0:T(8,128)(2,1)S(1)}, bf16[1536,576]{1,0:T(8,128)(2,1)}, u32[]{:S(2)}) copy-start(bf16[1536,576]{1,0:T(8,128)(2,1)} %all-gather.2.cloned.1.call-done) | copy-start | bytes 5308420
  66.9 3.9 %copy-start.2 = (bf16[32,512,128]{2,1,0:T(8,128)(2,1)S(1)}, bf16[32,512,128]{2,1,0:T(8,128)(2,1)}, u32[]{:S(2)}) copy-start(bf16[32,512,128]{2,1,0:T(8,128)(2,1)} %param.16) | copy-start | bytes 12582916
Sparse Core Ops, SparseCore 0:
  10.3 45.7 all-gather.1
where the time goes:
time: 81.7 us; the launch traced here: 81.2 us
  matrix products  27.7 us (34%)
  between operations  15 us (18%)
  local copies, waits for them, and re-layouts  9.05 us (11%)
  blocking collectives  8.31 us (10%)
  other arithmetic  7.63 us (9%)
  starting transfers between devices  7.47 us (9%)
  waiting for transfers between devices  6.08 us (7%)
    psum x1, blocking collectives, body(): raw = lax.psum(raw_part.astype(jnp.bfloat16), 'head').astype(jnp.float32)  8.31 us
    all_to_all x1, starting transfers between devices, body(): lax.all_to_all(by_slot, 'ctx', split_axis=0, concat_axis=1, tiled=True)  7.43 us
    dot_general x1, matrix products, body(): scores = jnp.dot(rows, piece.T, preferred_element_type=jnp.float32) * scale  7.2 us
    dot_general x2, matrix products, absorb(): jnp.einsum(form, query[..., :NOPE], w_uk, preferred_element_type=jnp.floa...  5.8 us
    all_gather x1, waiting for transfers between devices, body(): piece = lax.all_gather(prompt_latent, 'ctx', axis=0, tiled=True)  5.39 us
    dot_general x1, matrix products, body(): jnp.dot(probs.astype(jnp.bfloat16), piece[:, :KV_RANK], preferred_element...  3.83 us
    reduce_sum x1, other arithmetic, body(): total = jnp.sum(probs, axis=1)  3.53 us
    dot_general x1, matrix products, body(): jnp.dot(hidden_new.reshape(steps_here * owned, model_cols), w_down, prefe...  3.33 us
  transfers between devices with their start and end apart: 2, of which 1 were waited for; matrix products, arithmetic and copies ran while one was open for 30% of the time, Pallas kernels for 0%

commit v1 on v0

v1 whole, which is shorter than its diff:
```python
import functools

import jax
import jax.numpy as jnp
from jax import lax
from jax.experimental import pallas as pl
from jax.experimental.pallas import tpu as pltpu
from jax.sharding import PartitionSpec as P

KV_RANK = 512
ROPE = 64
NOPE = 128
LOG2E = 1.4426950408889634
LOW = -1e30
MESH = pl.DeviceIdType.MESH


def nt_dot(a, b):
    return lax.dot_general(a, b, (((1,), (1,)), ((), ())), preferred_element_type=jnp.float32)


def nn_dot(a, b):
    return jnp.dot(a, b, preferred_element_type=jnp.float32)


def kernel(
    dims,
    prompt, query, span, w_uk, w_uv, dlat, owner, lengths, hidden, w_down, gain,
    out_p, out_d,
    lat, qv, uk, uv, down, hid, dl, bys, keys, absp, absd, part, parts,
    lat_send, lat_recv, cache_send, cache_recv, swap_send, swap_recv, raw_send, raw_recv, load,
):
    n, nh, nz, ny, own, ppd, steps = dims
    heads = uk.shape[0]
    queries = absp.shape[1]
    chunk = lat.shape[1]
    group = n // nh
    me = lax.axis_index("ctx")
    hx = lax.axis_index("head")
    c = lax.rem(me, 2)
    y = lax.rem(me // 2, ny)
    z = me // (2 * ny)

    def at(zz, yy, cc):
        return (lax.rem(z + zz, nz) * ny + lax.rem(y + yy, ny)) * 2 + lax.rem(c + cc, 2)

    loads = [
        pltpu.make_async_copy(src, dst, load.at[i])
        for i, (src, dst) in enumerate(
            ((prompt, lat.at[me]), (dlat, dl), (hidden, hid), (w_down, down), (query, qv), (w_uk, uk), (w_uv, uv))
        )
    ]
    for copy in loads:
        copy.start()

    barrier = pltpu.get_barrier_semaphore()
    for k in range(1, n):
        pl.semaphore_signal(barrier, inc=1, device_id=(lax.rem(me + k, n), hx), device_id_type=MESH)
    for k in range(1, nh):
        pl.semaphore_signal(barrier, inc=1, device_id=(me, lax.rem(hx + k, nh)), device_id_type=MESH)
    pl.semaphore_wait(barrier, n - 1 + nh - 1)

    sent = []

    def send(shard, target, src=None):
        copy = pltpu.make_async_remote_copy(
            src_ref=lat.at[shard] if src is None else src,
            dst_ref=lat.at[shard],
            send_sem=lat_send.at[len(sent)],
            recv_sem=lat_recv.at[shard],
            device_id=(target, hx),
            device_id_type=MESH,
        )
        copy.start()
        sent.append(copy)

    def arrived(shard):
        pltpu.make_async_remote_copy(
            src_ref=lat.at[shard], dst_ref=lat.at[shard], send_sem=lat_send.at[0],
            recv_sem=lat_recv.at[shard], device_id=(me, hx), device_id_type=MESH,
        ).wait_recv()

    for dy in range(1, ny):
        send(me, at(0, dy, 0), prompt)
    for dz in range(1, nz):
        send(me, at(dz, 0, 0), prompt)
    send(me, at(0, 0, 1), prompt)

    loads[1].wait()
    rows = dl.shape[0]
    to = lax.broadcasted_iota(jnp.int32, (rows, rows), 0)
    of = lax.broadcasted_iota(jnp.int32, (rows, rows), 1)
    pick = (owner[...] == to // ppd) & (to % ppd == of % ppd)
    picked = nn_dot(jnp.where(pick, 1.0, 0.0).astype(jnp.bfloat16), dl[...])
    bys[...] = picked.astype(jnp.bfloat16).reshape(bys.shape)
    slot_in = hx * group + me // nh

    def cache_copy(k):
        target = lax.rem(me + k, n)
        return pltpu.make_async_remote_copy(
            src_ref=bys.at[target], dst_ref=keys.at[slot_in], send_sem=cache_send.at[k],
            recv_sem=cache_recv.at[me // nh], device_id=(target, hx), device_id_type=MESH,
        )

    mine = lax.rem(me, nh) == hx

    @pl.when(mine)
    def _():
        for k in range(1, n):
            cache_copy(k).start()
        keys[slot_in] = bys[me]

    loads[2].wait()
    loads[3].wait()
    part[...] = nn_dot(hid[...], down[...])
    parts[hx] = part[...]

    def raw_copy(k):
        return pltpu.make_async_remote_copy(
            src_ref=part, dst_ref=parts.at[hx], send_sem=raw_send.at[k], recv_sem=raw_recv.at[hx],
            device_id=(me, lax.rem(hx + k, nh)), device_id_type=MESH,
        )

    for k in range(1, nh):
        raw_copy(k).start()

    def absorb(h, _):
        q = qv[h]
        front = nn_dot(q[:, :NOPE], uk[h]).astype(jnp.bfloat16)
        absp[h, :, :KV_RANK] = front[:queries]
        absd[h, :, :KV_RANK] = front[queries:]
        absp[h, :, KV_RANK:] = q[:queries, NOPE:]
        absd[h, :, KV_RANK:] = q[queries:, NOPE:]
        return 0

    loads[4].wait()
    loads[5].wait()
    loads[0].wait()
    per = -(-heads // (nz - 1))
    for dz in range(1, nz):
        shard = at(dz, 0, 0)
        arrived(shard)
        for dy in range(1, ny):
            send(shard, at(0, dy, 0))
        send(shard, at(0, 0, 1))
        lax.fori_loop(min(heads, (dz - 1) * per), min(heads, dz * per), absorb, 0)
    for dz in range(nz):
        for dy in range(1, ny):
            shard = at(dz, dy, 0)
            arrived(shard)
            send(shard, at(0, 0, 1))

    for g in range(group):
        @pl.when(g * nh + hx != me)
        def _(g=g):
            pltpu.make_async_remote_copy(
                src_ref=bys.at[0], dst_ref=keys.at[hx * group + g], send_sem=cache_send.at[0],
                recv_sem=cache_recv.at[g], device_id=(me, hx), device_id_type=MESH,
            ).wait_recv()

    def swap_copy(k, col):
        here = keys.at[pl.ds(col * group, group)]
        return pltpu.make_async_remote_copy(
            src_ref=here, dst_ref=here, send_sem=swap_send.at[k], recv_sem=swap_recv.at[col],
            device_id=(me, lax.rem(hx + k, nh)), device_id_type=MESH,
        )

    for k in range(1, nh):
        swap_copy(k, hx).start()

    for dz in range(nz):
        for dy in range(ny):
            arrived(at(dz, dy, 1))
    loads[6].wait()

    factor = (NOPE + ROPE) ** (-0.5) * LOG2E
    first = span[0] + me * queries
    total = n * chunk
    per_step = max(1, 256 // queries)
    while heads % per_step:
        per_step -= 1
    spot = lax.broadcasted_iota(jnp.int32, (queries, total), 1)
    limit = first + lax.broadcasted_iota(jnp.int32, (queries, total), 0)
    veto = jnp.where(spot <= limit, 0.0, LOW)

    def attend(i, _):
        h0 = i * per_step
        q = absp[pl.ds(h0, per_step)].reshape(per_step * queries, absp.shape[2])
        k = lat[...].reshape(total, lat.shape[2])
        s = nt_dot(q, k).reshape(per_step, queries, total) + veto[None]
        s = s.reshape(per_step * queries, total)
        m = jnp.max(s, axis=1, keepdims=True)
        p = jnp.exp2((s - m) * factor)
        norm = jnp.sum(p, axis=1, keepdims=True)
        mixed = (nn_dot(p.astype(jnp.bfloat16), k[:, :KV_RANK]) / norm).astype(jnp.bfloat16)
        for j in range(per_step):
            o = nn_dot(mixed[j * queries : (j + 1) * queries], uv[h0 + j])
            out_p[h0 + j] = o.astype(jnp.bfloat16)
        return 0

    lax.fori_loop(0, heads // per_step, attend, 0)

    for k in range(1, nh):
        peer = lax.rem(hx + k, nh)
        pltpu.make_async_remote_copy(
            src_ref=part, dst_ref=parts.at[peer], send_sem=raw_send.at[0], recv_sem=raw_recv.at[peer],
            device_id=(me, hx), device_id_type=MESH,
        ).wait_recv()
        swap_copy(0, peer).wait_recv()
    raw = parts[0]
    for k in range(1, nh):
        raw = raw + parts[k]
    front = raw[:, :KV_RANK]
    scaling = lax.rsqrt(jnp.mean(front * front, axis=1, keepdims=True) + 1e-06)
    keys[n, :, :KV_RANK] = (front * scaling * gain[...]).astype(jnp.bfloat16)
    keys[n, :, KV_RANK:] = raw[:, KV_RANK:].astype(jnp.bfloat16)

    block = own * ppd
    news = steps * own
    kcount = (n + 1) * block
    kid = lax.broadcasted_iota(jnp.int32, (news, kcount), 1)
    rid = lax.broadcasted_iota(jnp.int32, (news, kcount), 0)
    place = kid // block
    inside = kid % block
    source = (place % group) * nh + place // group
    slot = inside // ppd
    position = source * ppd + inside % ppd
    length = jnp.zeros_like(kid)
    for r in range(own):
        length = jnp.where(slot == r, lengths[r], length)
    cached_ok = (slot == rid % own) & (position < length)
    new_ok = (inside % own == rid % own) & (inside // own <= rid // own)
    veto_d = jnp.where(jnp.where(place < n, jnp.where(cached_ok, 1, 0), jnp.where(new_ok, 1, 0)) > 0, 0.0, LOW)

    dper = min(heads, 8)

    def attend_d(i, _):
        h0 = i * dper
        q = absd[pl.ds(h0, dper)].reshape(dper * news, absd.shape[2])
        k = keys[...].reshape(kcount, keys.shape[2])
        s = (nt_dot(q, k).reshape(dper, news, kcount) + veto_d[None]).reshape(dper * news, kcount)
        m = jnp.max(s, axis=1, keepdims=True)
        p = jnp.exp2((s - m) * factor)
        norm = jnp.sum(p, axis=1, keepdims=True)
        mixed = (nn_dot(p.astype(jnp.bfloat16), k[:, :KV_RANK]) / norm).astype(jnp.bfloat16)
        for j in range(dper):
            out_d[h0 + j] = nn_dot(mixed[j * news : (j + 1) * news], uv[h0 + j]).astype(jnp.bfloat16)
        return 0

    lax.fori_loop(0, heads // dper, attend_d, 0)

    for copy in sent:
        copy.wait_send()
    for k in range(1, nh):
        raw_copy(k).wait_send()
        swap_copy(k, hx).wait_send()

    @pl.when(mine)
    def _():
        for k in range(1, n):
            cache_copy(k).wait_send()


def body(
    n, nh,
    prompt_latent, prefill_query, span_start, w_uk, w_uv, decode_latent, owner_slot, lengths,
    hidden_new, decode_query, w_down, kv_gain,
):
    heads = w_uk.shape[0]
    queries = prefill_query.shape[0]
    chunk, width = prompt_latent.shape
    steps, own, cols = hidden_new.shape
    requests, ppd, _ = decode_latent.shape
    news = steps * own
    chips = n // 2
    ny = 1
    while ny * ny * 4 <= chips:
        ny *= 2
    nz = chips // ny
    query = jnp.concatenate(
        [prefill_query, decode_query.reshape(news, heads, decode_query.shape[3])], axis=0
    ).transpose(1, 0, 2)
    dlat = decode_latent.reshape(requests * ppd, width)
    owner = jnp.repeat(owner_slot, ppd)[None, :]
    hidden = hidden_new.reshape(news, cols)
    bf = jnp.bfloat16
    hbm = pl.BlockSpec(memory_space=pl.ANY)
    vmem = pl.BlockSpec(memory_space=pltpu.VMEM)
    smem = pl.BlockSpec(memory_space=pltpu.SMEM)
    dma = pltpu.SemaphoreType.DMA
    block = own * ppd
    out_p, out_d = pl.pallas_call(
        functools.partial(kernel, (n, nh, nz, ny, own, ppd, steps)),
        out_shape=(
            jax.ShapeDtypeStruct((heads, queries, w_uv.shape[2]), bf),
            jax.ShapeDtypeStruct((heads, news, w_uv.shape[2]), bf),
        ),
        in_specs=[hbm, hbm, smem, hbm, hbm, hbm, vmem, smem, hbm, hbm, vmem],
        out_specs=(vmem, vmem),
        scratch_shapes=[
            pltpu.VMEM((n, chunk, width), bf),
            pltpu.VMEM(query.shape, bf),
            pltpu.VMEM(w_uk.shape, bf),
            pltpu.VMEM(w_uv.shape, bf),
            pltpu.VMEM(w_down.shape, bf),
            pltpu.VMEM(hidden.shape, bf),
            pltpu.VMEM(dlat.shape, bf),
            pltpu.VMEM((n, block, width), bf),
            pltpu.VMEM((n + 1, block, width), bf),
            pltpu.VMEM((heads, queries, width), bf),
            pltpu.VMEM((heads, news, width), bf),
            pltpu.VMEM((news, width), jnp.float32),
            pltpu.VMEM((nh, news, width), jnp.float32),
            dma((2 * n,)), dma((n,)), dma((n,)), dma((n // nh,)),
            dma((nh,)), dma((nh,)), dma((nh,)), dma((nh,)), dma((7,)),
        ],
        compiler_params=pltpu.CompilerParams(
            collective_id=0, has_side_effects=True, vmem_limit_bytes=56 * 1024 * 1024
        ),
        cost_estimate=pl.CostEstimate(
            flops=2 * heads * queries * n * chunk * (width + KV_RANK),
            bytes_accessed=2 * (w_uk.size + w_uv.size + w_down.size + query.size),
            transcendentals=heads * queries * n * chunk,
        ),
    )(prompt_latent, query, span_start, w_uk, w_uv, dlat, owner, lengths, hidden, w_down, kv_gain[None, :])
    decode_out = out_d.reshape(heads, steps, own, -1).transpose(1, 2, 0, 3)
    return (out_p.transpose(1, 0, 2), decode_out)


def solution(mesh):
    in_specs = (
        P("ctx", None),
        P("ctx", "head", None),
        P(),
        P("head", None, None),
        P("head", None, None),
        P(None, "ctx", None),
        P(),
        P("ctx"),
        P(None, "ctx", "head"),
        P(None, "ctx", "head", None),
        P("head", None),
        P(),
    )
    out_specs = (P("ctx", "head", None), P(None, "ctx", "head", None))
    n, nh = mesh.shape["ctx"], mesh.shape["head"]
    return jax.shard_map(
        functools.partial(body, n, nh), mesh=mesh, in_specs=in_specs, out_specs=out_specs, check_vma=False
    )
```

time: 81.7 us -> 69.4 us (0.85)
  the two profiles are of different devices: /device:TPU:0 before, /device:TPU:15 now
where the time goes in v1:
time: 69.4 us; the launch traced here: 68.9 us
  Pallas kernels  48.2 us (69%)
  local copies, waits for them, and re-layouts  18 us (26%)
  other arithmetic  1.33 us (2%)
  between operations  1.29 us (2%)
    pallas_call x1, Pallas kernels, body(): pl.pallas_call(functools.partial(kernel, (n, nh, nz, ny, own, ppd, steps)...  48.2 us
    unnamed x3, local copies, waits for them, and re-layouts  10.5 us
    reshape x1, local copies, waits for them, and re-layouts, body(): dlat = decode_latent.reshape(requests * ppd, width)  1.85 us
    reshape x1, local copies, waits for them, and re-layouts, body(): decode_out = out_d.reshape(heads, steps, own, -1).transpose(1, 2, 0, 3)  1.59 us
    reshape x1, local copies, waits for them, and re-layouts, body(): hidden = hidden_new.reshape(news, cols)  1.57 us

profile of v1, /device:TPU:15, one launch (start us, length us, event | category | flops | bytes accessed | tf_op | source)
XLA Modules:
  0.0 68.9 jit_solution(11066642238132511441)
XLA Ops:
  1.3 0.7 %broadcast_in_dim.6 = s32[64,4]{1,0:T(8,128)S(1)} broadcast(s32[64]{0:T(128)} %param.18), dimensions={0} | broadcast | bytes 1280 | tf_op jit(solution)/shard_map/broadcast_in_dim | solution.py:284
  2.0 0.7 broadcast_in_dim_reshape.3.owner
  2.7 1.6 %reshape.18.hidden = bf16[16,3584]{1,0:T(8,128)(2,1)} reshape(bf16[4,4,3584]{2,1,0:T(4,128)(2,1)} %param.20) | data formatting | bytes 229376 | tf_op jit(solution)/shard_map/reshape | solution.py:285
  4.3 1.1 %copy.24 = bf16[16,32,192]{2,0,1:T(8,128)(2,1)S(1)} copy(bf16[16,32,192]{2,1,0:T(8,128)(2,1)} %bitcast.10) | data formatting | bytes 393216 | tf_op jit(solution)/shard_map/reshape | solution.py:281
  5.4 1.9 %reshape.17.dlat = bf16[256,576]{1,0:T(8,128)(2,1)} reshape(bf16[64,4,576]{2,1,0:T(4,128)(2,1)} %param.17) | data formatting | bytes 589824 | tf_op jit(solution)/shard_map/reshape | solution.py:283
  7.2 1.8 %copy.20 = bf16[64,32,192]{2,0,1:T(8,128)(2,1)S(1)} copy(bf16[64,32,192]{2,1,0:T(8,128)(2,1)} %param.13) | data formatting | bytes 1572864 | tf_op args[1]
  9.0 1.3 %maximum_bitcast_fusion.query = bf16[32,80,192]{2,1,0:T(8,128)(2,1)} fusion(bf16[16,32,192]{2,0,1:T(8,128)(2,1)S(1)} %copy.24, bf16[64,32,192]{2,0,1:T(8,128)(2,1)S(1)} %copy.20), kind=kLoop, calls=%fused_computation | loop fusion | flops 1966080 | bytes 1966080 | tf_op jit(solution)/shard_map/transpose | solution.py:282
  10.4 6.5 %copy.21.w_down = bf16[3584,576]{1,0:T(8,128)(2,1)} copy(bf16[3584,576]{0,1:T(8,128)(2,1)} %param.22) | data formatting | bytes 8257536 | tf_op args[10]
  16.9 48.2 %shard_map.131 = (bf16[32,64,128]{2,1,0:T(8,128)(2,1)}, bf16[32,16,128]{2,1,0:T(8,128)(2,1)}) custom-call(bf16[96,576]{1,0:T(8,128)(2,1)} %prompt.1, bf16[32,80,192]{2,1,0:T(8,128)(2,1)} %maximum_bitcast_fusion.query, s32[1]{0:T(128)S(6)} %copy.27.span, bf16[32,128,512]{2,1,0:T(8,128)(2,1)} %w_uk.1, bf16[32,512,128]{2,1,0:T(8,128)(2,1)} %w_uv.1, ...), custom_call_target="tpu_custom_call" | custom-call | flops 6845104128 | bytes 13500416 | tf_op jit(solution)/shard_map/pallas_call | solution.py:292
  65.1 2.2 %copy.23 = bf16[64,32,128]{2,1,0:T(8,128)(2,1)} copy(bf16[64,32,128]{2,0,1:T(8,128)(2,1)} %bitcast.9) | data formatting | bytes 1048576
  67.3 1.6 %copy.26 = bf16[32,4,4,128]{3,0,2,1:T(8,128)(2,1)} copy(bf16[32,4,4,128]{3,2,1,0:T(4,128)(2,1)} %bitcast.12) | data formatting | bytes 262144 | tf_op jit(solution)/shard_map/reshape | solution.py:326

commit v2 on v1

--- a/solution.py
+++ b/solution.py
@@ -25,9 +25,9 @@
 
 def kernel(
     dims,
-    prompt, query, span, w_uk, w_uv, dlat, owner, lengths, hidden, w_down, gain,
+    prompt, query, dquery, span, w_uk, w_uv, dlat, owner, lengths, hidden, w_down, gain,
     out_p, out_d,
-    lat, qv, uk, uv, down, hid, dl, bys, keys, absp, absd, part, parts,
+    lat, lat_t, veto, qv, dqv, uk, uv, down, hid, dl, bys, keys, absp, absd, part, parts, top, total, acc,
     lat_send, lat_recv, cache_send, cache_recv, swap_send, swap_recv, raw_send, raw_recv, load,
 ):
     n, nh, nz, ny, own, ppd, steps = dims
@@ -35,6 +35,7 @@
     queries = absp.shape[1]
     chunk = lat.shape[1]
     group = n // nh
+    plane = n // ny
     me = lax.axis_index("ctx")
     hx = lax.axis_index("head")
     c = lax.rem(me, 2)
@@ -44,10 +45,16 @@
     def at(zz, yy, cc):
         return (lax.rem(z + zz, nz) * ny + lax.rem(y + yy, ny)) * 2 + lax.rem(c + cc, 2)
 
+    def place_of(zz, dy, cc):
+        return dy * plane + lax.rem(z + zz, nz) * 2 + lax.rem(c + cc, 2)
+
     loads = [
         pltpu.make_async_copy(src, dst, load.at[i])
         for i, (src, dst) in enumerate(
-            ((prompt, lat.at[me]), (dlat, dl), (hidden, hid), (w_down, down), (query, qv), (w_uk, uk), (w_uv, uv))
+            (
+                (prompt, lat.at[place_of(0, 0, 0)]), (dlat, dl), (hidden, hid), (w_down, down),
+                (query, qv), (dquery, dqv), (w_uk, uk), (w_uv, uv),
+            )
         )
     ]
     for copy in loads:
@@ -62,36 +69,38 @@
 
     sent = []
 
-    def send(shard, target, src=None):
+    def send(src, place, target):
         copy = pltpu.make_async_remote_copy(
-            src_ref=lat.at[shard] if src is None else src,
-            dst_ref=lat.at[shard],
-            send_sem=lat_send.at[len(sent)],
-            recv_sem=lat_recv.at[shard],
-            device_id=(target, hx),
-            device_id_type=MESH,
+            src_ref=src, dst_ref=lat.at[place], send_sem=lat_send.at[len(sent)],
+            recv_sem=lat_recv.at[place], device_id=(target, hx), device_id_type=MESH,
         )
         copy.start()
         sent.append(copy)
 
-    def arrived(shard):
+    def arrived(place):
         pltpu.make_async_remote_copy(
-            src_ref=lat.at[shard], dst_ref=lat.at[shard], send_sem=lat_send.at[0],
-            recv_sem=lat_recv.at[shard], device_id=(me, hx), device_id_type=MESH,
+            src_ref=lat.at[place], dst_ref=lat.at[place], send_sem=lat_send.at[0],
+            recv_sem=lat_recv.at[place], device_id=(me, hx), device_id_type=MESH,
         ).wait_recv()
 
+    for dz in range(1, nz):
+        send(prompt, place_of(0, 0, 0), at(dz, 0, 0))
     for dy in range(1, ny):
-        send(me, at(0, dy, 0), prompt)
-    for dz in range(1, nz):
-        send(me, at(dz, 0, 0), prompt)
-    send(me, at(0, 0, 1), prompt)
+        send(prompt, place_of(0, ny - dy, 0), at(0, dy, 0))
+    send(prompt, place_of(0, 0, 0), at(0, 0, 1))
 
     loads[1].wait()
-    rows = dl.shape[0]
-    to = lax.broadcasted_iota(jnp.int32, (rows, rows), 0)
-    of = lax.broadcasted_iota(jnp.int32, (rows, rows), 1)
-    pick = (owner[...] == to // ppd) & (to % ppd == of % ppd)
-    picked = nn_dot(jnp.where(pick, 1.0, 0.0).astype(jnp.bfloat16), dl[...])
+    requests = dl.shape[0]
+    rows = requests * ppd
+    to = lax.broadcasted_iota(jnp.int32, (rows, requests), 0)
+    slot_to = (to // (own * ppd)) * own + to % own
+    place_to = (to // own) % ppd
+    pick = owner[...] == slot_to
+    picked = jnp.zeros((rows, dl.shape[2]), jnp.float32)
+    flat = dl[...].astype(jnp.float32)
+    for p in range(ppd):
+        one = jnp.where(pick & (place_to == p), 1.0, 0.0).astype(jnp.bfloat16)
+        picked = picked + nn_dot(one, flat[:, p, :].astype(jnp.bfloat16))
     bys[...] = picked.astype(jnp.bfloat16).reshape(bys.shape)
     slot_in = hx * group + me // nh
 
@@ -112,7 +121,7 @@
 
     loads[2].wait()
     loads[3].wait()
-    part[...] = nn_dot(hid[...], down[...])
+    part[...] = nt_dot(hid[...].reshape(steps * own, hid.shape[2]), down[...])
     parts[hx] = part[...]
 
     def raw_copy(k):
@@ -125,30 +134,87 @@
         raw_copy(k).start()
 
     def absorb(h, _):
-        q = qv[h]
-        front = nn_dot(q[:, :NOPE], uk[h]).astype(jnp.bfloat16)
-        absp[h, :, :KV_RANK] = front[:queries]
-        absd[h, :, :KV_RANK] = front[queries:]
-        absp[h, :, KV_RANK:] = q[:queries, NOPE:]
-        absd[h, :, KV_RANK:] = q[queries:, NOPE:]
+        for q, out in ((qv[h], absp), (dqv[h], absd)):
+            out[h, :, :KV_RANK] = nn_dot(q[:, :NOPE], uk[h]).astype(jnp.bfloat16)
+            out[h, :, KV_RANK:] = q[:, NOPE:]
         return 0
 
     loads[4].wait()
     loads[5].wait()
+    loads[6].wait()
     loads[0].wait()
     per = -(-heads // (nz - 1))
     for dz in range(1, nz):
-        shard = at(dz, 0, 0)
+        shard = place_of(dz, 0, 0)
         arrived(shard)
         for dy in range(1, ny):
-            send(shard, at(0, dy, 0))
-        send(shard, at(0, 0, 1))
+            send(lat.at[shard], place_of(dz, ny - dy, 0), at(0, dy, 0))
+        send(lat.at[shard], shard, at(0, 0, 1))
         lax.fori_loop(min(heads, (dz - 1) * per), min(heads, dz * per), absorb, 0)
+
+    factor = (NOPE + ROPE) ** (-0.5) * LOG2E
+    lanes = veto.shape[1]
+    per_step = lanes // queries
+    ahead = lax.broadcasted_iota(jnp.int32, (chunk, lanes), 1) % queries - lax.broadcasted_iota(
+        jnp.int32, (chunk, lanes), 0
+    )
+    first = span[0] + me * queries
+    for dy in range(ny):
+        for k in range(plane):
+            base = ((k // 2) * ny + lax.rem(y + dy, ny)) * 2 + k % 2
+            place = dy * plane + k
+            veto[pl.ds(place * chunk, chunk), :] = jnp.where(ahead >= base * chunk - first, 0.0, LOW)
+
+    together = 4 if (heads // per_step) % 4 == 0 else 1
+    depth = plane * chunk
+
+    def attend(dy):
+        k = lat[dy * plane : (dy + 1) * plane].reshape(depth, lat.shape[2])
+        lat_t[...] = k[:, :KV_RANK].T
+
+        def one_round(i, _):
+            groups = [i * together + j for j in range(together)]
+            scores = []
+            for g in groups:
+                q = absp[pl.ds(g * per_step, per_step)].reshape(lanes, absp.shape[2])
+                k = lat[dy * plane : (dy + 1) * plane].reshape(depth, lat.shape[2])
+                scores.append(nt_dot(k, q))
+            for g, s in zip(groups, scores):
+                s = s + veto[dy * depth : (dy + 1) * depth, :]
+                m = jnp.max(s, axis=0, keepdims=True)
+                if dy:
+                    before = top[g]
+                    m = jnp.maximum(m, before)
+                p = jnp.exp2((s - m) * factor)
+                norm = jnp.sum(p, axis=0, keepdims=True)
+                mixed = nn_dot(lat_t[...], p.astype(jnp.bfloat16))
+                if dy:
+                    fade = jnp.exp2((before - m) * factor)
+                    norm = norm + total[g] * fade
+                    mixed = mixed + acc[g] * fade
+                if dy < ny - 1:
+                    top[g] = m
+                    total[g] = norm
+                    acc[g] = mixed
+                else:
+                    mixed = (mixed / norm).T.astype(jnp.bfloat16)
+                    for j in range(per_step):
+                        h = g * per_step + j
+                        o = nn_dot(mixed[j * queries : (j + 1) * queries], uv[h])
+                        out_p[h] = o.astype(jnp.bfloat16)
+            return 0
+
+        lax.fori_loop(0, heads // per_step // together, one_round, 0)
+
     for dz in range(nz):
-        for dy in range(1, ny):
-            shard = at(dz, dy, 0)
+        arrived(place_of(dz, 0, 1))
+    attend(0)
+
+    for dy in range(1, ny):
+        for dz in range(nz):
+            shard = place_of(dz, dy, 0)
             arrived(shard)
-            send(shard, at(0, 0, 1))
+            send(lat.at[shard], shard, at(0, 0, 1))
 
     for g in range(group):
         @pl.when(g * nh + hx != me)
@@ -168,37 +234,11 @@
     for k in range(1, nh):
         swap_copy(k, hx).start()
 
-    for dz in range(nz):
-        for dy in range(ny):
-            arrived(at(dz, dy, 1))
-    loads[6].wait()
-
-    factor = (NOPE + ROPE) ** (-0.5) * LOG2E
-    first = span[0] + me * queries
-    total = n * chunk
-    per_step = max(1, 256 // queries)
-    while heads % per_step:
-        per_step -= 1
-    spot = lax.broadcasted_iota(jnp.int32, (queries, total), 1)
-    limit = first + lax.broadcasted_iota(jnp.int32, (queries, total), 0)
-    veto = jnp.where(spot <= limit, 0.0, LOW)
-
-    def attend(i, _):
-        h0 = i * per_step
-        q = absp[pl.ds(h0, per_step)].reshape(per_step * queries, absp.shape[2])
-        k = lat[...].reshape(total, lat.shape[2])
-        s = nt_dot(q, k).reshape(per_step, queries, total) + veto[None]
-        s = s.reshape(per_step * queries, total)
-        m = jnp.max(s, axis=1, keepdims=True)
-        p = jnp.exp2((s - m) * factor)
-        norm = jnp.sum(p, axis=1, keepdims=True)
-        mixed = (nn_dot(p.astype(jnp.bfloat16), k[:, :KV_RANK]) / norm).astype(jnp.bfloat16)
-        for j in range(per_step):
-            o = nn_dot(mixed[j * queries : (j + 1) * queries], uv[h0 + j])
-            out_p[h0 + j] = o.astype(jnp.bfloat16)
-        return 0
-
-    lax.fori_loop(0, heads // per_step, attend, 0)
+    loads[7].wait()
+    for dy in range(1, ny):
+        for dz in range(nz):
+            arrived(place_of(dz, dy, 1))
+        attend(dy)
 
     for k in range(1, nh):
         peer = lax.rem(hx + k, nh)
@@ -223,16 +263,17 @@
     place = kid // block
     inside = kid % block
     source = (place % group) * nh + place // group
-    slot = inside // ppd
-    position = source * ppd + inside % ppd
+    slot = inside % own
+    position = source * ppd + inside // own
     length = jnp.zeros_like(kid)
     for r in range(own):
         length = jnp.where(slot == r, lengths[r], length)
-    cached_ok = (slot == rid % own) & (position < length)
-    new_ok = (inside % own == rid % own) & (inside // own <= rid // own)
-    veto_d = jnp.where(jnp.where(place < n, jnp.where(cached_ok, 1, 0), jnp.where(new_ok, 1, 0)) > 0, 0.0, LOW)
-
-    dper = min(heads, 8)
+    cached_ok = position < length
+    new_ok = inside // own <= rid // own
+    fits = jnp.where(place < n, jnp.where(cached_ok, 1, 0), jnp.where(new_ok, 1, 0))
+    veto_d = jnp.where((fits > 0) & (slot == rid % own), 0.0, LOW)
+
+    dper = min(heads, 16)
 
     def attend_d(i, _):
         h0 = i * dper
@@ -277,12 +318,13 @@
     while ny * ny * 4 <= chips:
         ny *= 2
     nz = chips // ny
-    query = jnp.concatenate(
-        [prefill_query, decode_query.reshape(news, heads, decode_query.shape[3])], axis=0
-    ).transpose(1, 0, 2)
-    dlat = decode_latent.reshape(requests * ppd, width)
-    owner = jnp.repeat(owner_slot, ppd)[None, :]
-    hidden = hidden_new.reshape(news, cols)
+    query = prefill_query.transpose(1, 0, 2)
+    dquery = decode_query.reshape(news, heads, decode_query.shape[3]).transpose(1, 0, 2)
+    lanes = queries * (256 // queries)
+    while lanes > queries and heads % (lanes // queries):
+        lanes -= queries
+    groups = heads * queries // lanes
+    depth = n // ny * chunk
     bf = jnp.bfloat16
     hbm = pl.BlockSpec(memory_space=pl.ANY)
     vmem = pl.BlockSpec(memory_space=pltpu.VMEM)
@@ -295,24 +337,30 @@
             jax.ShapeDtypeStruct((heads, queries, w_uv.shape[2]), bf),
             jax.ShapeDtypeStruct((heads, news, w_uv.shape[2]), bf),
         ),
-        in_specs=[hbm, hbm, smem, hbm, hbm, hbm, vmem, smem, hbm, hbm, vmem],
+        in_specs=[hbm, hbm, hbm, smem, hbm, hbm, hbm, vmem, smem, hbm, hbm, vmem],
         out_specs=(vmem, vmem),
         scratch_shapes=[
             pltpu.VMEM((n, chunk, width), bf),
+            pltpu.VMEM((KV_RANK, depth), bf),
+            pltpu.VMEM((n * chunk, lanes), jnp.float32),
             pltpu.VMEM(query.shape, bf),
+            pltpu.VMEM(dquery.shape, bf),
             pltpu.VMEM(w_uk.shape, bf),
             pltpu.VMEM(w_uv.shape, bf),
-            pltpu.VMEM(w_down.shape, bf),
-            pltpu.VMEM(hidden.shape, bf),
-            pltpu.VMEM(dlat.shape, bf),
+            pltpu.VMEM((width, cols), bf),
+            pltpu.VMEM(hidden_new.shape, bf),
+            pltpu.VMEM(decode_latent.shape, bf),
             pltpu.VMEM((n, block, width), bf),
             pltpu.VMEM((n + 1, block, width), bf),
             pltpu.VMEM((heads, queries, width), bf),
             pltpu.VMEM((heads, news, width), bf),
             pltpu.VMEM((news, width), jnp.float32),
             pltpu.VMEM((nh, news, width), jnp.float32),
+            pltpu.VMEM((groups, 1, lanes), jnp.float32),
+            pltpu.VMEM((groups, 1, lanes), jnp.float32),
+            pltpu.VMEM((groups, KV_RANK, lanes), jnp.float32),
             dma((2 * n,)), dma((n,)), dma((n,)), dma((n // nh,)),
-            dma((nh,)), dma((nh,)), dma((nh,)), dma((nh,)), dma((7,)),
+            dma((nh,)), dma((nh,)), dma((nh,)), dma((nh,)), dma((8,)),
         ],
         compiler_params=pltpu.CompilerParams(
             collective_id=0, has_side_effects=True, vmem_limit_bytes=56 * 1024 * 1024
@@ -322,7 +370,10 @@
             bytes_accessed=2 * (w_uk.size + w_uv.size + w_down.size + query.size),
             transcendentals=heads * queries * n * chunk,
         ),
-    )(prompt_latent, query, span_start, w_uk, w_uv, dlat, owner, lengths, hidden, w_down, kv_gain[None, :])
+    )(
+        prompt_latent, query, dquery, span_start, w_uk, w_uv, decode_latent, owner_slot[None, :], lengths,
+        hidden_new, w_down.T, kv_gain[None, :],
+    )
     decode_out = out_d.reshape(heads, steps, own, -1).transpose(1, 2, 0, 3)
     return (out_p.transpose(1, 0, 2), decode_out)
 

time: 69.4 us -> 61.1 us (0.88)
  the two profiles are of different devices: /device:TPU:15 before, /device:TPU:8 now
where the time goes in v2:
time: 61.1 us; the launch traced here: 60.1 us
  Pallas kernels  50.4 us (82%)
  local copies, waits for them, and re-layouts  8.37 us (14%)
  between operations  1.29 us (2%)
    pallas_call x1, Pallas kernels, body(): pl.pallas_call(functools.partial(kernel, (n, nh, nz, ny, own, ppd, steps)...  50.4 us
    unnamed x2, local copies, waits for them, and re-layouts  4.97 us
    reshape x1, local copies, waits for them, and re-layouts, body(): decode_query.reshape(news, heads, decode_query.shape[3]).transpose(1, 0, 2)  1.8 us
    reshape x1, local copies, waits for them, and re-layouts, body(): decode_out = out_d.reshape(heads, steps, own, -1).transpose(1, 2, 0, 3)  1.59 us

profile of v2, /device:TPU:8, one launch (start us, length us, event | category | flops | bytes accessed | tf_op | source)
XLA Modules:
  0.0 60.1 jit_solution(9816079099724721913)
XLA Ops:
  1.3 1.8 %copy.23 = bf16[16,32,192]{2,0,1:T(8,128)(2,1)} copy(bf16[16,32,192]{2,1,0:T(8,128)(2,1)} %bitcast.17) | data formatting | bytes 393216 | tf_op jit(solution)/shard_map/reshape | solution.py:322
  3.1 2.8 %copy.22 = bf16[64,32,192]{2,0,1:T(8,128)(2,1)} copy(bf16[64,32,192]{2,1,0:T(8,128)(2,1)} %param.13) | data formatting | bytes 1572864 | tf_op args[1]
  5.9 50.4 %shard_map.131 = (bf16[32,64,128]{2,1,0:T(8,128)(2,1)}, bf16[32,16,128]{2,1,0:T(8,128)(2,1)}) custom-call(bf16[96,576]{1,0:T(8,128)(2,1)} %prompt.1, bf16[32,64,192]{2,1,0:T(8,128)(2,1)} %bitcast.15, bf16[32,16,192]{2,1,0:T(8,128)(2,1)} %bitcast.18, s32[1]{0:T(128)S(6)} %copy.25.span, bf16[32,128,512]{2,1,0:T(8,128)(2,1)} %w_uk.1, ...), custom_call_target="tpu_custom_call" | custom-call | flops 6845104128 | bytes 13303808 | tf_op jit(solution)/shard_map/pallas_call | solution.py:334
  56.3 2.2 %copy.17 = bf16[64,32,128]{2,1,0:T(8,128)(2,1)} copy(bf16[64,32,128]{2,0,1:T(8,128)(2,1)} %bitcast.16) | data formatting | bytes 1048576
  58.5 1.6 %copy.24 = bf16[32,4,4,128]{3,0,2,1:T(8,128)(2,1)} copy(bf16[32,4,4,128]{3,2,1,0:T(4,128)(2,1)} %bitcast.20) | data formatting | bytes 262144 | tf_op jit(solution)/shard_map/reshape | solution.py:377

commit v3 on v2

v3 whole, which is shorter than its diff:
```python
import functools

import jax
import jax.numpy as jnp
from jax import lax
from jax.experimental import pallas as pl
from jax.experimental.pallas import tpu as pltpu
from jax.sharding import PartitionSpec as P

KV_RANK = 512
ROPE = 64
NOPE = 128
LOG2E = 1.4426950408889634
LOW = -1e30
MESH = pl.DeviceIdType.MESH


def nt_dot(a, b):
    return lax.dot_general(a, b, (((1,), (1,)), ((), ())), preferred_element_type=jnp.float32)


def nn_dot(a, b):
    return jnp.dot(a, b, preferred_element_type=jnp.float32)


def gather(
    dims,
    prompt, query, dquery, w_uk, dlat, owner, hidden, w_down, gain,
    lat, keys, absp, absd,
    qv, dqv, qt, uk, down, hid, dl, bys, part, parts,
    lat_send, lat_recv, cache_send, cache_recv, swap_send, swap_recv, raw_send, raw_recv, load,
):
    n, nh, nz, ny, own, ppd, steps = dims
    heads = uk.shape[0]
    queries = absp.shape[1]
    chunk = lat.shape[1]
    group = n // nh
    me = lax.axis_index("ctx")
    hx = lax.axis_index("head")
    c = lax.rem(me, 2)
    y = lax.rem(me // 2, ny)
    z = me // (2 * ny)

    def at(zz, yy, cc):
        return (lax.rem(z + zz, nz) * ny + lax.rem(y + yy, ny)) * 2 + lax.rem(c + cc, 2)

    loads = [
        pltpu.make_async_copy(src, dst, load.at[i])
        for i, (src, dst) in enumerate(
            (
                (prompt, lat.at[me]), (dlat, dl), (hidden, hid), (w_down, down),
                (query, qv), (dquery, dqv), (w_uk, uk),
            )
        )
    ]
    for copy in loads:
        copy.start()

    barrier = pltpu.get_barrier_semaphore()
    for k in range(1, n):
        pl.semaphore_signal(barrier, inc=1, device_id=(lax.rem(me + k, n), hx), device_id_type=MESH)
    for k in range(1, nh):
        pl.semaphore_signal(barrier, inc=1, device_id=(me, lax.rem(hx + k, nh)), device_id_type=MESH)
    pl.semaphore_wait(barrier, n - 1 + nh - 1)

    sent = []

    def send(src, place, target):
        copy = pltpu.make_async_remote_copy(
            src_ref=src, dst_ref=lat.at[place], send_sem=lat_send.at[len(sent)],
            recv_sem=lat_recv.at[place], device_id=(target, hx), device_id_type=MESH,
        )
        copy.start()
        sent.append(copy)

    def arrived(place):
        pltpu.make_async_remote_copy(
            src_ref=lat.at[place], dst_ref=lat.at[place], send_sem=lat_send.at[0],
            recv_sem=lat_recv.at[place], device_id=(me, hx), device_id_type=MESH,
        ).wait_recv()

    for dz in range(1, nz):
        send(prompt, me, at(dz, 0, 0))
    for dy in range(1, ny):
        send(prompt, me, at(0, dy, 0))
    send(prompt, me, at(0, 0, 1))

    loads[1].wait()
    requests = dl.shape[0]
    rows = requests * ppd
    to = lax.broadcasted_iota(jnp.int32, (rows, requests), 0)
    slot_to = (to // (own * ppd)) * own + to % own
    place_to = (to // own) % ppd
    pick = owner[...] == slot_to
    picked = jnp.zeros((rows, dl.shape[2]), jnp.float32)
    flat = dl[...].astype(jnp.float32)
    for p in range(ppd):
        one = jnp.where(pick & (place_to == p), 1.0, 0.0).astype(jnp.bfloat16)
        picked = picked + nn_dot(one, flat[:, p, :].astype(jnp.bfloat16))
    bys[...] = picked.astype(jnp.bfloat16).reshape(bys.shape)
    slot_in = hx * group + me // nh

    def cache_copy(k):
        target = lax.rem(me + k, n)
        return pltpu.make_async_remote_copy(
            src_ref=bys.at[target], dst_ref=keys.at[slot_in], send_sem=cache_send.at[k],
            recv_sem=cache_recv.at[me // nh], device_id=(target, hx), device_id_type=MESH,
        )

    mine = lax.rem(me, nh) == hx

    @pl.when(mine)
    def _():
        for k in range(1, n):
            cache_copy(k).start()
        keys[slot_in] = bys[me]

    loads[2].wait()
    loads[3].wait()
    part[...] = nt_dot(hid[...].reshape(steps * own, hid.shape[2]), down[...])
    parts[hx] = part[...]

    def raw_copy(k):
        return pltpu.make_async_remote_copy(
            src_ref=part, dst_ref=parts.at[hx], send_sem=raw_send.at[k], recv_sem=raw_recv.at[hx],
            device_id=(me, lax.rem(hx + k, nh)), device_id_type=MESH,
        )

    for k in range(1, nh):
        raw_copy(k).start()

    def absorb(h, _):
        q = qt[h]
        front = nn_dot(q[:, :NOPE], uk[h]).astype(jnp.bfloat16)
        absp[h, :, :KV_RANK] = front[:queries]
        absd[h, :, :KV_RANK] = front[queries:]
        absp[h, :, KV_RANK:] = q[:queries, NOPE:]
        absd[h, :, KV_RANK:] = q[queries:, NOPE:]
        return 0

    loads[4].wait()
    loads[5].wait()

    def turn(i, _):
        at_q = pl.multiple_of(i * 16, 16)
        qt[:, pl.ds(at_q, 16), :] = jnp.swapaxes(qv[pl.ds(at_q, 16)], 0, 1)
        return 0

    lax.fori_loop(0, queries // 16, turn, 0)
    news = steps * own
    qt[:, queries:, :] = jnp.swapaxes(dqv[...].reshape(news, heads, dqv.shape[3]), 0, 1)
    loads[6].wait()
    loads[0].wait()
    per = -(-heads // (nz - 1))
    for dz in range(1, nz):
        shard = at(dz, 0, 0)
        arrived(shard)
        for dy in range(1, ny):
            send(lat.at[shard], shard, at(0, dy, 0))
        send(lat.at[shard], shard, at(0, 0, 1))
        lax.fori_loop(min(heads, (dz - 1) * per), min(heads, dz * per), absorb, 0)
    for dz in range(nz):
        for dy in range(1, ny):
            shard = at(dz, dy, 0)
            arrived(shard)
            send(lat.at[shard], shard, at(0, 0, 1))

    for g in range(group):
        @pl.when(g * nh + hx != me)
        def _(g=g):
            pltpu.make_async_remote_copy(
                src_ref=bys.at[0], dst_ref=keys.at[hx * group + g], send_sem=cache_send.at[0],
                recv_sem=cache_recv.at[g], device_id=(me, hx), device_id_type=MESH,
            ).wait_recv()

    def swap_copy(k, col):
        here = keys.at[pl.ds(col * group, group)]
        return pltpu.make_async_remote_copy(
            src_ref=here, dst_ref=here, send_sem=swap_send.at[k], recv_sem=swap_recv.at[col],
            device_id=(me, lax.rem(hx + k, nh)), device_id_type=MESH,
        )

    for k in range(1, nh):
        swap_copy(k, hx).start()

    for k in range(1, nh):
        peer = lax.rem(hx + k, nh)
        pltpu.make_async_remote_copy(
            src_ref=part, dst_ref=parts.at[peer], send_sem=raw_send.at[0], recv_sem=raw_recv.at[peer],
            device_id=(me, hx), device_id_type=MESH,
        ).wait_recv()
        swap_copy(0, peer).wait_recv()
    raw = parts[0]
    for k in range(1, nh):
        raw = raw + parts[k]
    front = raw[:, :KV_RANK]
    scaling = lax.rsqrt(jnp.mean(front * front, axis=1, keepdims=True) + 1e-06)
    keys[n, :, :KV_RANK] = (front * scaling * gain[...]).astype(jnp.bfloat16)
    keys[n, :, KV_RANK:] = raw[:, KV_RANK:].astype(jnp.bfloat16)

    for dz in range(nz):
        for dy in range(ny):
            arrived(at(dz, dy, 1))
    for copy in sent:
        copy.wait_send()
    for k in range(1, nh):
        raw_copy(k).wait_send()
        swap_copy(k, hx).wait_send()

    @pl.when(mine)
    def _():
        for k in range(1, n):
            cache_copy(k).wait_send()


def attention(
    dims,
    span, lengths, lat, keys, absp, absd, uv,
    out_p, out_d,
    lat_t, veto,
):
    n, nh, own, ppd, steps = dims
    heads, queries, width = absp.shape
    chunk = lat.shape[1]
    total = n * chunk
    group = n // nh
    block = own * ppd
    news = steps * own
    kcount = (n + 1) * block
    factor = (NOPE + ROPE) ** (-0.5) * LOG2E
    lanes = veto.shape[1]
    per_step = lanes // queries
    first = span[0] + lax.axis_index("ctx") * queries

    @pl.when(pl.program_id(0) == 0)
    def _():
        lat_t[...] = lat[...].reshape(total, width)[:, :KV_RANK].T
        spot = lax.broadcasted_iota(jnp.int32, (total, lanes), 0)
        limit = first + lax.broadcasted_iota(jnp.int32, (total, lanes), 1) % queries
        veto[...] = jnp.where(spot <= limit, 0.0, LOW)

    done = []
    scores = []
    for g in range(heads // per_step):
        q = absp[g * per_step : (g + 1) * per_step].reshape(lanes, width)
        scores.append(nt_dot(lat[...].reshape(total, width), q))
    for g, s in enumerate(scores):
        s = s + veto[...]
        m = jnp.max(s, axis=0, keepdims=True)
        p = jnp.exp2((s - m) * factor)
        norm = jnp.sum(p, axis=0, keepdims=True)
        mixed = (nn_dot(lat_t[...], p.astype(jnp.bfloat16)) / norm).T.astype(jnp.bfloat16)
        for j in range(per_step):
            done.append(nn_dot(mixed[j * queries : (j + 1) * queries], uv[g * per_step + j]))
    out_p[...] = jnp.swapaxes(jnp.stack(done), 0, 1).astype(jnp.bfloat16)

    kid = lax.broadcasted_iota(jnp.int32, (news, kcount), 1)
    rid = lax.broadcasted_iota(jnp.int32, (news, kcount), 0)
    place = kid // block
    inside = kid % block
    source = (place % group) * nh + place // group
    slot = inside % own
    position = source * ppd + inside // own
    length = jnp.zeros_like(kid)
    for r in range(own):
        length = jnp.where(slot == r, lengths[r], length)
    cached_ok = position < length
    new_ok = inside // own <= rid // own
    fits = jnp.where(place < n, jnp.where(cached_ok, 1, 0), jnp.where(new_ok, 1, 0))
    veto_d = jnp.where((fits > 0) & (slot == rid % own), 0.0, LOW)

    q = absd[...].reshape(heads * news, width)
    k = keys[...].reshape(kcount, width)
    s = (nt_dot(q, k).reshape(heads, news, kcount) + veto_d[None]).reshape(heads * news, kcount)
    m = jnp.max(s, axis=1, keepdims=True)
    p = jnp.exp2((s - m) * factor)
    norm = jnp.sum(p, axis=1, keepdims=True)
    mixed = (nn_dot(p.astype(jnp.bfloat16), k[:, :KV_RANK]) / norm).astype(jnp.bfloat16)
    done = [nn_dot(mixed[j * news : (j + 1) * news], uv[j]) for j in range(heads)]
    out_d[...] = jnp.swapaxes(jnp.stack(done), 0, 1).astype(jnp.bfloat16).reshape(out_d.shape)


def body(
    n, nh,
    prompt_latent, prefill_query, span_start, w_uk, w_uv, decode_latent, owner_slot, lengths,
    hidden_new, decode_query, w_down, kv_gain,
):
    heads = w_uk.shape[0]
    queries = prefill_query.shape[0]
    chunk, width = prompt_latent.shape
    steps, own, cols = hidden_new.shape
    requests, ppd, _ = decode_latent.shape
    news = steps * own
    chips = n // 2
    ny = 1
    while ny * ny * 4 <= chips:
        ny *= 2
    nz = chips // ny
    bf = jnp.bfloat16
    hbm = pl.BlockSpec(memory_space=pl.ANY)
    vmem = pl.BlockSpec(memory_space=pltpu.VMEM)
    smem = pl.BlockSpec(memory_space=pltpu.SMEM)
    dma = pltpu.SemaphoreType.DMA
    block = own * ppd
    size = prefill_query.shape[2]
    lat, keys, absp, absd = pl.pallas_call(
        functools.partial(gather, (n, nh, nz, ny, own, ppd, steps)),
        out_shape=(
            jax.ShapeDtypeStruct((n, chunk, width), bf),
            jax.ShapeDtypeStruct((n + 1, block, width), bf),
            jax.ShapeDtypeStruct((heads, queries, width), bf),
            jax.ShapeDtypeStruct((heads, news, width), bf),
        ),
        in_specs=[hbm, hbm, hbm, hbm, hbm, vmem, hbm, hbm, vmem],
        out_specs=(vmem, vmem, vmem, vmem),
        scratch_shapes=[
            pltpu.VMEM(prefill_query.shape, bf),
            pltpu.VMEM(decode_query.shape, bf),
            pltpu.VMEM((heads, queries + news, size), bf),
            pltpu.VMEM(w_uk.shape, bf),
            pltpu.VMEM((width, cols), bf),
            pltpu.VMEM(hidden_new.shape, bf),
            pltpu.VMEM(decode_latent.shape, bf),
            pltpu.VMEM((n, block, width), bf),
            pltpu.VMEM((news, width), jnp.float32),
            pltpu.VMEM((nh, news, width), jnp.float32),
            dma((2 * n,)), dma((n,)), dma((n,)), dma((n // nh,)),
            dma((nh,)), dma((nh,)), dma((nh,)), dma((nh,)), dma((7,)),
        ],
        compiler_params=pltpu.CompilerParams(
            collective_id=0, has_side_effects=True, vmem_limit_bytes=40 * 1024 * 1024
        ),
        cost_estimate=pl.CostEstimate(
            flops=2 * heads * (queries + news) * NOPE * KV_RANK + 2 * news * w_down.size,
            bytes_accessed=2 * (w_uk.size + w_down.size + prefill_query.size),
            transcendentals=0,
        ),
    )(
        prompt_latent, prefill_query, decode_query, w_uk, decode_latent, owner_slot[None, :],
        hidden_new, w_down.T, kv_gain[None, :],
    )
    per_call = min(heads, 8)
    lanes = queries * min(per_call, max(1, 256 // queries))
    vdim = w_uv.shape[2]

    def whole(shape):
        return pl.BlockSpec(shape, lambda i: (0,) * len(shape))

    return pl.pallas_call(
        functools.partial(attention, (n, nh, own, ppd, steps)),
        grid=(heads // per_call,),
        out_shape=(
            jax.ShapeDtypeStruct((queries, heads, vdim), bf),
            jax.ShapeDtypeStruct((steps, own, heads, vdim), bf),
        ),
        in_specs=[
            smem, smem, whole(lat.shape), whole(keys.shape),
            pl.BlockSpec((per_call, queries, width), lambda i: (i, 0, 0)),
            pl.BlockSpec((per_call, news, width), lambda i: (i, 0, 0)),
            pl.BlockSpec((per_call, KV_RANK, vdim), lambda i: (i, 0, 0)),
        ],
        out_specs=(
            pl.BlockSpec((queries, per_call, vdim), lambda i: (0, i, 0)),
            pl.BlockSpec((steps, own, per_call, vdim), lambda i: (0, 0, i, 0)),
        ),
        scratch_shapes=[
            pltpu.VMEM((KV_RANK, n * chunk), bf),
            pltpu.VMEM((n * chunk, lanes), jnp.float32),
        ],
        compiler_params=pltpu.CompilerParams(vmem_limit_bytes=56 * 1024 * 1024),
        cost_estimate=pl.CostEstimate(
            flops=2 * heads * queries * n * chunk * (width + KV_RANK),
            bytes_accessed=2 * (w_uv.size + absp.size + lat.size),
            transcendentals=heads * queries * n * chunk,
        ),
    )(span_start, lengths, lat, keys, absp, absd, w_uv)


def solution(mesh):
    in_specs = (
        P("ctx", None),
        P("ctx", "head", None),
        P(),
        P("head", None, None),
        P("head", None, None),
        P(None, "ctx", None),
        P(),
        P("ctx"),
        P(None, "ctx", "head"),
        P(None, "ctx", "head", None),
        P("head", None),
        P(),
    )
    out_specs = (P("ctx", "head", None), P(None, "ctx", "head", None))
    n, nh = mesh.shape["ctx"], mesh.shape["head"]
    return jax.shard_map(
        functools.partial(body, n, nh), mesh=mesh, in_specs=in_specs, out_specs=out_specs, check_vma=False
    )
```

time: 61.1 us -> 77.3 us (1.27)
  Pallas kernels: 50.4 us -> 62.3 us
  local copies, waits for them, and re-layouts: 8.37 us -> 12.8 us
    pallas_call x1 -> x2, Pallas kernels: 50.4 us -> 62.3 us  [the longest x1 34.1 us: body(): pl.pallas_call(functools.partial(gather, (n, nh, nz, ny, own, ppd, steps)...]
    unnamed x2 -> x24, local copies, waits for them, and re-layouts: 4.97 us -> 12.8 us
    reshape x2 -> x0, local copies, waits for them, and re-layouts: 3.39 us -> none  [the longest x1 1.8 us: body(): decode_query.reshape(news, heads, decode_query.shape[3]).transpose(1, 0, 2)]
where the time goes in v3:
time: 77.3 us; the launch traced here: 76.4 us
  Pallas kernels  62.3 us (81%)
  local copies, waits for them, and re-layouts  12.8 us (17%)
  between operations  1.31 us (2%)
    pallas_call x1, Pallas kernels, body(): pl.pallas_call(functools.partial(gather, (n, nh, nz, ny, own, ppd, steps)...  34.1 us
    pallas_call x1, Pallas kernels, body(): pl.pallas_call(functools.partial(attention, (n, nh, own, ppd, steps)), gr...  28.2 us
    unnamed x24, local copies, waits for them, and re-layouts  12.8 us

profile of v3, /device:TPU:8, one launch (start us, length us, event | category | flops | bytes accessed | tf_op | source)
XLA Modules:
  0.0 76.4 jit_solution(718719770022119081)
XLA Ops:
  1.3 0.0 copy-start
  1.3 2.2 %copy-done = bf16[3584,576]{0,1:T(8,128)(2,1)S(1)} copy-done((bf16[3584,576]{0,1:T(8,128)(2,1)S(1)}, bf16[3584,576]{0,1:T(8,128)(2,1)}, u32[]{:S(2)}) %copy-start) | copy-done | bytes 4128792
  3.4 0.0 copy-start.1
  3.5 1.2 %copy-done.1 = bf16[64,32,192]{2,1,0:T(8,128)(2,1)S(1)} copy-done((bf16[64,32,192]{2,1,0:T(8,128)(2,1)S(1)}, bf16[64,32,192]{2,1,0:T(8,128)(2,1)}, u32[]{:S(2)}) %copy-start.1) | copy-done | bytes 786456
  4.7 1.0 %copy-done.2 = bf16[64,4,576]{2,1,0:T(4,128)(2,1)S(1)} copy-done((bf16[64,4,576]{2,1,0:T(4,128)(2,1)S(1)}, bf16[64,4,576]{2,1,0:T(4,128)(2,1)}, u32[]{:S(2)}) %copy-start.2) | copy-done | bytes 294936
  5.6 0.0 copy-start.3
  5.6 0.9 %copy-done.3 = bf16[4,4,32,192]{3,2,1,0:T(8,128)(2,1)S(1)} copy-done((bf16[4,4,32,192]{3,2,1,0:T(8,128)(2,1)S(1)}, bf16[4,4,32,192]{3,2,1,0:T(8,128)(2,1)}, u32[]{:S(2)}) %copy-start.3) | copy-done | bytes 196632
  6.6 0.0 copy-start.4
  6.6 0.9 %copy-done.4 = bf16[96,576]{1,0:T(8,128)(2,1)S(1)} copy-done((bf16[96,576]{1,0:T(8,128)(2,1)S(1)}, bf16[96,576]{1,0:T(8,128)(2,1)}, u32[]{:S(2)}) %copy-start.4) | copy-done | bytes 110616
  7.5 0.0 copy-start.5
  7.5 0.9 %copy-done.5 = bf16[4,4,3584]{2,1,0:T(4,128)(2,1)S(1)} copy-done((bf16[4,4,3584]{2,1,0:T(4,128)(2,1)S(1)}, bf16[4,4,3584]{2,1,0:T(4,128)(2,1)}, u32[]{:S(2)}) %copy-start.5) | copy-done | bytes 114712
  8.4 0.0 copy-start.6
  8.4 0.7 copy-done.6
  9.1 0.0 copy-start.7
  9.1 0.7 copy-done.7
  9.7 34.1 %shard_map.131 = (bf16[16,96,576]{2,1,0:T(8,128)(2,1)S(1)}, bf16[17,16,576]{2,1,0:T(8,128)(2,1)S(1)}, bf16[32,64,576]{2,1,0:T(8,128)(2,1)S(1)}, bf16[32,16,576]{2,1,0:T(8,128)(2,1)S(1)}) custom-call(bf16[96,576]{1,0:T(8,128)(2,1)S(1)} %copy-done.4, bf16[64,32,192]{2,1,0:T(8,128)(2,1)S(1)} %copy-done.1, bf16[4,4,32,192]{3,2,1,0:T(8,128)(2,1)S(1)} %copy-done.3, ...), custom_call_target="tpu_custom_call" | custom-call | flops 401604608 | bytes 9109504 | tf_op jit(solution)/shard_map/pallas_call | solution.py:306
  43.8 0.0 copy-start.8
  43.9 1.5 %copy-done.8 = bf16[32,64,576]{2,1,0:T(8,128)(2,1)} copy-done((bf16[32,64,576]{2,1,0:T(8,128)(2,1)}, bf16[32,64,576]{2,1,0:T(8,128)(2,1)S(1)}, u32[]{:S(2)}) %copy-start.8) | copy-done | bytes 2359320
  45.4 0.0 copy-start.9
  45.4 1.3 %copy-done.9 = bf16[16,96,576]{2,1,0:T(8,128)(2,1)} copy-done((bf16[16,96,576]{2,1,0:T(8,128)(2,1)}, bf16[16,96,576]{2,1,0:T(8,128)(2,1)S(1)}, u32[]{:S(2)}) %copy-start.9) | copy-done | bytes 1769496
  46.6 0.8 %copy-done.10 = bf16[32,16,576]{2,1,0:T(8,128)(2,1)} copy-done((bf16[32,16,576]{2,1,0:T(8,128)(2,1)}, bf16[32,16,576]{2,1,0:T(8,128)(2,1)S(1)}, u32[]{:S(2)}) %copy-start.10) | copy-done | bytes 589848
  47.5 0.0 copy-start.11
  47.5 0.7 copy-done.11
  48.2 28.2 %shard_map.132 = (bf16[64,32,128]{2,1,0:T(8,128)(2,1)}, bf16[4,4,32,128]{3,2,1,0:T(8,128)(2,1)}) custom-call(s32[1]{0:T(128)S(6)} %copy.14.span, s32[4]{0:T(128)} %lengths.1, bf16[16,96,576]{2,1,0:T(8,128)(2,1)} %copy-done.9, bf16[17,16,576]{2,1,0:T(8,128)(2,1)} %copy-done.11, bf16[32,64,576]{2,1,0:T(8,128)(2,1)} %copy-done.8, ...), custom_call_target="tpu_custom_call" | custom-call | flops 6845104128 | bytes 8323072 | tf_op jit(solution)/shard_map/pallas_call | solution.py:349
  (2 shorter events, 0.0 us)
Async XLA Ops:
  1.3 2.2 %copy-start = (bf16[3584,576]{0,1:T(8,128)(2,1)S(1)}, bf16[3584,576]{0,1:T(8,128)(2,1)}, u32[]{:S(2)}) copy-start(bf16[3584,576]{0,1:T(8,128)(2,1)} %param.22) | copy-start | bytes 12386308
  3.4 1.2 %copy-start.1 = (bf16[64,32,192]{2,1,0:T(8,128)(2,1)S(1)}, bf16[64,32,192]{2,1,0:T(8,128)(2,1)}, u32[]{:S(2)}) copy-start(bf16[64,32,192]{2,1,0:T(8,128)(2,1)} %query.1) | copy-start | bytes 2359300
  4.7 1.0 %copy-start.2 = (bf16[64,4,576]{2,1,0:T(4,128)(2,1)S(1)}, bf16[64,4,576]{2,1,0:T(4,128)(2,1)}, u32[]{:S(2)}) copy-start(bf16[64,4,576]{2,1,0:T(4,128)(2,1)} %dlat.1) | copy-start | bytes 884740
  5.6 0.9 %copy-start.3 = (bf16[4,4,32,192]{3,2,1,0:T(8,128)(2,1)S(1)}, bf16[4,4,32,192]{3,2,1,0:T(8,128)(2,1)}, u32[]{:S(2)}) copy-start(bf16[4,4,32,192]{3,2,1,0:T(8,128)(2,1)} %dquery.1) | copy-start | bytes 589828
  6.6 0.9 %copy-start.4 = (bf16[96,576]{1,0:T(8,128)(2,1)S(1)}, bf16[96,576]{1,0:T(8,128)(2,1)}, u32[]{:S(2)}) copy-start(bf16[96,576]{1,0:T(8,128)(2,1)} %prompt.1) | copy-start | bytes 331780
  7.5 0.9 %copy-start.5 = (bf16[4,4,3584]{2,1,0:T(4,128)(2,1)S(1)}, bf16[4,4,3584]{2,1,0:T(4,128)(2,1)}, u32[]{:S(2)}) copy-start(bf16[4,4,3584]{2,1,0:T(4,128)(2,1)} %hidden.1) | copy-start | bytes 344068
  8.4 0.7 copy-start.6
  9.1 0.7 copy-start.7
  43.8 1.5 %copy-start.8 = (bf16[32,64,576]{2,1,0:T(8,128)(2,1)}, bf16[32,64,576]{2,1,0:T(8,128)(2,1)S(1)}, u32[]{:S(2)}) copy-start(bf16[32,64,576]{2,1,0:T(8,128)(2,1)S(1)} %get-tuple-element.8.absp) | copy-start | bytes 7077892
  45.4 1.3 %copy-start.9 = (bf16[16,96,576]{2,1,0:T(8,128)(2,1)}, bf16[16,96,576]{2,1,0:T(8,128)(2,1)S(1)}, u32[]{:S(2)}) copy-start(bf16[16,96,576]{2,1,0:T(8,128)(2,1)S(1)} %get-tuple-element.6.lat) | copy-start | bytes 5308420
  46.6 0.8 %copy-start.10 = (bf16[32,16,576]{2,1,0:T(8,128)(2,1)}, bf16[32,16,576]{2,1,0:T(8,128)(2,1)S(1)}, u32[]{:S(2)}) copy-start(bf16[32,16,576]{2,1,0:T(8,128)(2,1)S(1)} %get-tuple-element.9.absd) | copy-start | bytes 1769476
  47.5 0.8 copy-start.11

commit v4 on v3

--- a/solution.py
+++ b/solution.py
@@ -65,25 +65,55 @@
 
     sent = []
 
-    def send(src, place, target):
+    def send(k, src, shard, target):
         copy = pltpu.make_async_remote_copy(
-            src_ref=src, dst_ref=lat.at[place], send_sem=lat_send.at[len(sent)],
-            recv_sem=lat_recv.at[place], device_id=(target, hx), device_id_type=MESH,
+            src_ref=src, dst_ref=lat.at[shard], send_sem=lat_send.at[k],
+            recv_sem=lat_recv.at[shard], device_id=target, device_id_type=MESH,
         )
         copy.start()
-        sent.append(copy)
-
-    def arrived(place):
+        sent.append((k, relay))
+
+    def arrived(shard):
         pltpu.make_async_remote_copy(
-            src_ref=lat.at[place], dst_ref=lat.at[place], send_sem=lat_send.at[0],
-            recv_sem=lat_recv.at[place], device_id=(me, hx), device_id_type=MESH,
+            src_ref=lat.at[shard], dst_ref=lat.at[shard], send_sem=lat_send.at[0],
+            recv_sem=lat_recv.at[shard], device_id=(me, hx), device_id_type=MESH,
         ).wait_recv()
 
-    for dz in range(1, nz):
-        send(prompt, me, at(dz, 0, 0))
-    for dy in range(1, ny):
-        send(prompt, me, at(0, dy, 0))
-    send(prompt, me, at(0, 0, 1))
+    first_half = max(1, nz // 2)
+    counts = [0, 0]
+    relay = 0
+
+    def forward(src, shard, dz, dy, to_y, to_x):
+        def push(target):
+            send(counts[relay], src, shard, target)
+            counts[relay] += 1
+
+        for k in range(1, ny) if to_y else ():
+            push((at(0, k, 0), hx))
+        for k in range(1, nh) if to_x else ():
+            push((me, lax.rem(hx + k, nh)))
+        push((at(0, 0, 1), hx))
+
+    def step(dz, dy):
+        nonlocal relay
+        for relay in (0, 1):
+            @pl.when(leads if relay == 0 else jnp.logical_not(leads))
+            def _():
+                shard = at(dz, dy, 0)
+                if dz or dy:
+                    arrived(shard)
+                src = lat.at[shard] if dz or dy else prompt
+                if relay == 0:
+                    if not dz and not dy:
+                        for k in range(1, nz):
+                            send(counts[0], src, shard, (at(k, 0, 0), hx))
+                            counts[0] += 1
+                    forward(src, shard, dz, dy, dy == 0, dz >= first_half if dy else dz > 0)
+                else:
+                    forward(src, shard, dz, dy, dy == 0 and dz < first_half, False)
+
+    leads = hx == c
+    step(0, 0)
 
     loads[1].wait()
     requests = dl.shape[0]
@@ -138,6 +168,7 @@
         absd[h, :, KV_RANK:] = q[queries:, NOPE:]
         return 0
 
+    step(1, 0)
     loads[4].wait()
     loads[5].wait()
 
@@ -151,19 +182,13 @@
     qt[:, queries:, :] = jnp.swapaxes(dqv[...].reshape(news, heads, dqv.shape[3]), 0, 1)
     loads[6].wait()
     loads[0].wait()
-    per = -(-heads // (nz - 1))
-    for dz in range(1, nz):
-        shard = at(dz, 0, 0)
-        arrived(shard)
-        for dy in range(1, ny):
-            send(lat.at[shard], shard, at(0, dy, 0))
-        send(lat.at[shard], shard, at(0, 0, 1))
-        lax.fori_loop(min(heads, (dz - 1) * per), min(heads, dz * per), absorb, 0)
+    per = -(-heads // max(1, nz - 2))
+    for dz in range(2, nz):
+        step(dz, 0)
+        lax.fori_loop(min(heads, (dz - 2) * per), min(heads, (dz - 1) * per), absorb, 0)
     for dz in range(nz):
         for dy in range(1, ny):
-            shard = at(dz, dy, 0)
-            arrived(shard)
-            send(lat.at[shard], shard, at(0, 0, 1))
+            step(dz, dy)
 
     for g in range(group):
         @pl.when(g * nh + hx != me)
@@ -201,8 +226,15 @@
     for dz in range(nz):
         for dy in range(ny):
             arrived(at(dz, dy, 1))
-    for copy in sent:
-        copy.wait_send()
+    for relay in (0, 1):
+        @pl.when(leads if relay == 0 else jnp.logical_not(leads))
+        def _():
+            for k, role in sent:
+                if role == relay:
+                    pltpu.make_async_remote_copy(
+                        src_ref=prompt, dst_ref=lat.at[me], send_sem=lat_send.at[k],
+                        recv_sem=lat_recv.at[me], device_id=(me, hx), device_id_type=MESH,
+                    ).wait_send()
     for k in range(1, nh):
         raw_copy(k).wait_send()
         swap_copy(k, hx).wait_send()
@@ -217,7 +249,7 @@
     dims,
     span, lengths, lat, keys, absp, absd, uv,
     out_p, out_d,
-    lat_t, veto,
+    lat_t, veto, score, weight,
 ):
     n, nh, own, ppd, steps = dims
     heads, queries, width = absp.shape
@@ -235,21 +267,31 @@
     @pl.when(pl.program_id(0) == 0)
     def _():
         lat_t[...] = lat[...].reshape(total, width)[:, :KV_RANK].T
-        spot = lax.broadcasted_iota(jnp.int32, (total, lanes), 0)
-        limit = first + lax.broadcasted_iota(jnp.int32, (total, lanes), 1) % queries
-        veto[...] = jnp.where(spot <= limit, 0.0, LOW)
-
-    done = []
-    scores = []
+        ahead = lax.broadcasted_iota(jnp.int32, (chunk, lanes), 1) % queries - lax.broadcasted_iota(
+            jnp.int32, (chunk, lanes), 0
+        )
+        for k in range(n):
+            veto[k * chunk : (k + 1) * chunk] = jnp.where(ahead >= k * chunk - first, 0.0, LOW)
+
+    rows = 64
     for g in range(heads // per_step):
         q = absp[g * per_step : (g + 1) * per_step].reshape(lanes, width)
-        scores.append(nt_dot(lat[...].reshape(total, width), q))
-    for g, s in enumerate(scores):
-        s = s + veto[...]
-        m = jnp.max(s, axis=0, keepdims=True)
-        p = jnp.exp2((s - m) * factor)
-        norm = jnp.sum(p, axis=0, keepdims=True)
-        mixed = (nn_dot(lat_t[...], p.astype(jnp.bfloat16)) / norm).T.astype(jnp.bfloat16)
+        score[g] = nt_dot(lat[...].reshape(total, width), q)
+    done = []
+    for g in range(heads // per_step):
+        top = jnp.full((8, lanes), LOW, jnp.float32)
+        for r in range(0, total, rows):
+            x = score[g, r : r + rows] + veto[r : r + rows]
+            score[g, r : r + rows] = x
+            top = jnp.maximum(top, jnp.max(x.reshape(rows // 8, 8, lanes), axis=0))
+        m = jnp.max(top, axis=0, keepdims=True)
+        norm = jnp.zeros((8, lanes), jnp.float32)
+        for r in range(0, total, rows):
+            p = jnp.exp2((score[g, r : r + rows] - m) * factor)
+            norm = norm + jnp.sum(p.reshape(rows // 8, 8, lanes), axis=0)
+            weight[g, r : r + rows] = p.astype(jnp.bfloat16)
+        norm = jnp.sum(norm, axis=0, keepdims=True)
+        mixed = (nn_dot(lat_t[...], weight[g]) / norm).T.astype(jnp.bfloat16)
         for j in range(per_step):
             done.append(nn_dot(mixed[j * queries : (j + 1) * queries], uv[g * per_step + j]))
     out_p[...] = jnp.swapaxes(jnp.stack(done), 0, 1).astype(jnp.bfloat16)
@@ -324,11 +366,11 @@
             pltpu.VMEM((n, block, width), bf),
             pltpu.VMEM((news, width), jnp.float32),
             pltpu.VMEM((nh, news, width), jnp.float32),
-            dma((2 * n,)), dma((n,)), dma((n,)), dma((n // nh,)),
+            dma((2 * n * nh,)), dma((n,)), dma((n,)), dma((n // nh,)),
             dma((nh,)), dma((nh,)), dma((nh,)), dma((nh,)), dma((7,)),
         ],
         compiler_params=pltpu.CompilerParams(
-            collective_id=0, has_side_effects=True, vmem_limit_bytes=40 * 1024 * 1024
+            collective_id=0, has_side_effects=True, vmem_limit_bytes=60 * 1024 * 1024
         ),
         cost_estimate=pl.CostEstimate(
             flops=2 * heads * (queries + news) * NOPE * KV_RANK + 2 * news * w_down.size,
@@ -366,8 +408,10 @@
         scratch_shapes=[
             pltpu.VMEM((KV_RANK, n * chunk), bf),
             pltpu.VMEM((n * chunk, lanes), jnp.float32),
+            pltpu.VMEM((per_call * queries // lanes, n * chunk, lanes), jnp.float32),
+            pltpu.VMEM((per_call * queries // lanes, n * chunk, lanes), bf),
         ],
-        compiler_params=pltpu.CompilerParams(vmem_limit_bytes=56 * 1024 * 1024),
+        compiler_params=pltpu.CompilerParams(vmem_limit_bytes=60 * 1024 * 1024),
         cost_estimate=pl.CostEstimate(
             flops=2 * heads * queries * n * chunk * (width + KV_RANK),
             bytes_accessed=2 * (w_uv.size + absp.size + lat.size),

time: 77.3 us -> 57.6 us (0.75)
  local copies, waits for them, and re-layouts: 12.8 us -> 0 us
  Pallas kernels: 62.3 us -> 55.4 us
    unnamed x24 -> x0, local copies, waits for them, and re-layouts: 12.8 us -> none
    pallas_call x1, Pallas kernels: 28.2 us -> 22.5 us  [body(): pl.pallas_call(functools.partial(attention, (n, nh, own, ppd, steps)), gr...]
    pallas_call x1, Pallas kernels: 34.1 us -> 32.9 us  [body(): pl.pallas_call(functools.partial(gather, (n, nh, nz, ny, own, ppd, steps)...]
where the time goes in v4:
time: 57.6 us; the launch traced here: 56.7 us
  Pallas kernels  55.4 us (96%)
  between operations  1.29 us (2%)
    pallas_call x1, Pallas kernels, body(): pl.pallas_call(functools.partial(gather, (n, nh, nz, ny, own, ppd, steps)...  32.9 us
    pallas_call x1, Pallas kernels, body(): pl.pallas_call(functools.partial(attention, (n, nh, own, ppd, steps)), gr...  22.5 us

profile of v4, /device:TPU:8, one launch (start us, length us, event | category | flops | bytes accessed | tf_op | source)
XLA Modules:
  0.0 56.7 jit_solution(5786063049524607952)
XLA Ops:
  1.3 32.9 %shard_map.131 = (bf16[16,96,576]{2,1,0:T(8,128)(2,1)}, bf16[17,16,576]{2,1,0:T(8,128)(2,1)}, bf16[32,64,576]{2,1,0:T(8,128)(2,1)}, bf16[32,16,576]{2,1,0:T(8,128)(2,1)}) custom-call(bf16[96,576]{1,0:T(8,128)(2,1)} %prompt.1, bf16[64,32,192]{2,1,0:T(8,128)(2,1)} %query.1, bf16[4,4,32,192]{3,2,1,0:T(8,128)(2,1)} %dquery.1, bf16[32,128,512]{2,1,0:T(8,128)(2,1)} %w_uk.1, ...), custom_call_target="tpu_custom_call" | custom-call | flops 401604608 | bytes 9109504 | tf_op jit(solution)/shard_map/pallas_call | solution.py:348
  34.2 22.5 %shard_map.132 = (bf16[64,32,128]{2,1,0:T(8,128)(2,1)}, bf16[4,4,32,128]{3,2,1,0:T(8,128)(2,1)}) custom-call(s32[1]{0:T(128)S(6)} %copy.14.span, s32[4]{0:T(128)} %lengths.1, bf16[16,96,576]{2,1,0:T(8,128)(2,1)} %get-tuple-element.6.lat, bf16[17,16,576]{2,1,0:T(8,128)(2,1)} %get-tuple-element.7.keys, bf16[32,64,576]{2,1,0:T(8,128)(2,1)} %get-tuple-element.8.absp, ...), custom_call_target="tpu_custom_call" | custom-call | flops 6845104128 | bytes 8323072 | tf_op jit(solution)/shard_map/pallas_call | solution.py:391

commit v5 on v4

--- a/solution.py
+++ b/solution.py
@@ -119,15 +119,16 @@
     requests = dl.shape[0]
     rows = requests * ppd
     to = lax.broadcasted_iota(jnp.int32, (rows, requests), 0)
-    slot_to = (to // (own * ppd)) * own + to % own
-    place_to = (to // own) % ppd
-    pick = owner[...] == slot_to
-    picked = jnp.zeros((rows, dl.shape[2]), jnp.float32)
-    flat = dl[...].astype(jnp.float32)
-    for p in range(ppd):
-        one = jnp.where(pick & (place_to == p), 1.0, 0.0).astype(jnp.bfloat16)
-        picked = picked + nn_dot(one, flat[:, p, :].astype(jnp.bfloat16))
-    bys[...] = picked.astype(jnp.bfloat16).reshape(bys.shape)
+    pick = jnp.where(owner[...] == (to // (own * ppd)) * own + to % own, 1.0, 0.0).astype(jnp.bfloat16)
+    spread = lax.broadcasted_iota(jnp.int32, (requests, rows), 1) // ppd == lax.broadcasted_iota(
+        jnp.int32, (requests, rows), 0
+    )
+    wide = nn_dot(pick, jnp.where(spread, 1.0, 0.0).astype(jnp.bfloat16))
+    place_to = (lax.broadcasted_iota(jnp.int32, (rows, rows), 0) // own) % ppd
+    same = lax.broadcasted_iota(jnp.int32, (rows, rows), 1) % ppd == place_to
+    wide = jnp.where(same, wide, 0.0).astype(jnp.bfloat16)
+    flat = dl[...].astype(jnp.float32).reshape(rows, dl.shape[2]).astype(jnp.bfloat16)
+    bys[...] = nn_dot(wide, flat).astype(jnp.bfloat16).reshape(bys.shape)
     slot_in = hx * group + me // nh
 
     def cache_copy(k):
@@ -147,7 +148,7 @@
 
     loads[2].wait()
     loads[3].wait()
-    part[...] = nt_dot(hid[...].reshape(steps * own, hid.shape[2]), down[...])
+    part[...] = nt_dot(down[...], hid[...].reshape(steps * own, hid.shape[2])).T
     parts[hx] = part[...]
 
     def raw_copy(k):
@@ -159,13 +160,24 @@
     for k in range(1, nh):
         raw_copy(k).start()
 
-    def absorb(h, _):
-        q = qt[h]
-        front = nn_dot(q[:, :NOPE], uk[h]).astype(jnp.bfloat16)
-        absp[h, :, :KV_RANK] = front[:queries]
-        absd[h, :, :KV_RANK] = front[queries:]
-        absp[h, :, KV_RANK:] = q[:queries, NOPE:]
-        absd[h, :, KV_RANK:] = q[queries:, NOPE:]
+    news = steps * own
+    pair = 2 if heads % 2 == 0 else 1
+
+    def absorb(i, _):
+        qs = [qt[i * pair + j] for j in range(pair)]
+        lefts = [
+            jnp.concatenate([q[:, :NOPE] if k == j else jnp.zeros_like(q[:, :NOPE]) for k in range(pair)], axis=1)
+            for j, q in enumerate(qs)
+        ]
+        right = uk[pl.ds(i * pair, pair)].reshape(pair * NOPE, KV_RANK)
+        front = nn_dot(jnp.concatenate(lefts, axis=0), right).astype(jnp.bfloat16)
+        for j, q in enumerate(qs):
+            h = i * pair + j
+            base = j * (queries + news)
+            absp[h, :, :KV_RANK] = front[base : base + queries]
+            absd[h, :, :KV_RANK] = front[base + queries : base + queries + news]
+            absp[h, :, KV_RANK:] = q[:queries, NOPE:]
+            absd[h, :, KV_RANK:] = q[queries:, NOPE:]
         return 0
 
     step(1, 0)
@@ -178,14 +190,16 @@
         return 0
 
     lax.fori_loop(0, queries // 16, turn, 0)
-    news = steps * own
     qt[:, queries:, :] = jnp.swapaxes(dqv[...].reshape(news, heads, dqv.shape[3]), 0, 1)
     loads[6].wait()
     loads[0].wait()
-    per = -(-heads // max(1, nz - 2))
+    pairs = heads // pair
+    per = -(-pairs // max(1, nz - 2))
     for dz in range(2, nz):
         step(dz, 0)
-        lax.fori_loop(min(heads, (dz - 2) * per), min(heads, (dz - 1) * per), absorb, 0)
+        low, high = min(pairs, (dz - 2) * per), min(pairs, (dz - 1) * per)
+        if high > low:
+            lax.fori_loop(low, high, absorb, 0, unroll=4 if (high - low) % 4 == 0 else 1)
     for dz in range(nz):
         for dy in range(1, ny):
             step(dz, dy)
@@ -249,7 +263,7 @@
     dims,
     span, lengths, lat, keys, absp, absd, uv,
     out_p, out_d,
-    lat_t, veto, score, weight,
+    lat_t, veto, score, weight, veto_d,
 ):
     n, nh, own, ppd, steps = dims
     heads, queries, width = absp.shape
@@ -272,12 +286,34 @@
         )
         for k in range(n):
             veto[k * chunk : (k + 1) * chunk] = jnp.where(ahead >= k * chunk - first, 0.0, LOW)
+        kid = lax.broadcasted_iota(jnp.int32, (news, kcount), 1)
+        rid = lax.broadcasted_iota(jnp.int32, (news, kcount), 0)
+        place = kid // block
+        inside = kid % block
+        source = (place % group) * nh + place // group
+        slot = inside % own
+        position = source * ppd + inside // own
+        length = jnp.zeros_like(kid)
+        for r in range(own):
+            length = jnp.where(slot == r, lengths[r], length)
+        cached_ok = position < length
+        new_ok = inside // own <= rid // own
+        fits = jnp.where(place < n, jnp.where(cached_ok, 1, 0), jnp.where(new_ok, 1, 0))
+        veto_d[...] = jnp.where((fits > 0) & (slot == rid % own), 0.0, LOW)
 
     rows = 64
     for g in range(heads // per_step):
         q = absp[g * per_step : (g + 1) * per_step].reshape(lanes, width)
         score[g] = nt_dot(lat[...].reshape(total, width), q)
-    done = []
+    q = absd[...].reshape(heads * news, width)
+    k = keys[...].reshape(kcount, width)
+    s = (nt_dot(q, k).reshape(heads, news, kcount) + veto_d[...][None]).reshape(heads * news, kcount)
+    m = jnp.max(s, axis=1, keepdims=True)
+    p = jnp.exp2((s - m) * factor)
+    norm = jnp.sum(p, axis=1, keepdims=True)
+    mixed_d = (nn_dot(p.astype(jnp.bfloat16), k[:, :KV_RANK]) / norm).astype(jnp.bfloat16)
+    done, done_d = [], []
+    pair = 2 if per_step % 2 == 0 else 1
     for g in range(heads // per_step):
         top = jnp.full((8, lanes), LOW, jnp.float32)
         for r in range(0, total, rows):
@@ -292,34 +328,19 @@
             weight[g, r : r + rows] = p.astype(jnp.bfloat16)
         norm = jnp.sum(norm, axis=0, keepdims=True)
         mixed = (nn_dot(lat_t[...], weight[g]) / norm).T.astype(jnp.bfloat16)
-        for j in range(per_step):
-            done.append(nn_dot(mixed[j * queries : (j + 1) * queries], uv[g * per_step + j]))
+        for j in range(0, per_step, pair):
+            h = g * per_step + j
+            left = jnp.concatenate(
+                [mixed[j * queries : (j + pair) * queries], mixed_d[h * news : (h + pair) * news]], axis=0
+            )
+            o = nn_dot(left, jnp.concatenate([uv[h + k] for k in range(pair)], axis=1))
+            vdim = uv.shape[2]
+            for k in range(pair):
+                mine = o[:, k * vdim : (k + 1) * vdim]
+                done.append(mine[k * queries : (k + 1) * queries])
+                done_d.append(mine[pair * queries + k * news : pair * queries + (k + 1) * news])
     out_p[...] = jnp.swapaxes(jnp.stack(done), 0, 1).astype(jnp.bfloat16)
-
-    kid = lax.broadcasted_iota(jnp.int32, (news, kcount), 1)
-    rid = lax.broadcasted_iota(jnp.int32, (news, kcount), 0)
-    place = kid // block
-    inside = kid % block
-    source = (place % group) * nh + place // group
-    slot = inside % own
-    position = source * ppd + inside // own
-    length = jnp.zeros_like(kid)
-    for r in range(own):
-        length = jnp.where(slot == r, lengths[r], length)
-    cached_ok = position < length
-    new_ok = inside // own <= rid // own
-    fits = jnp.where(place < n, jnp.where(cached_ok, 1, 0), jnp.where(new_ok, 1, 0))
-    veto_d = jnp.where((fits > 0) & (slot == rid % own), 0.0, LOW)
-
-    q = absd[...].reshape(heads * news, width)
-    k = keys[...].reshape(kcount, width)
-    s = (nt_dot(q, k).reshape(heads, news, kcount) + veto_d[None]).reshape(heads * news, kcount)
-    m = jnp.max(s, axis=1, keepdims=True)
-    p = jnp.exp2((s - m) * factor)
-    norm = jnp.sum(p, axis=1, keepdims=True)
-    mixed = (nn_dot(p.astype(jnp.bfloat16), k[:, :KV_RANK]) / norm).astype(jnp.bfloat16)
-    done = [nn_dot(mixed[j * news : (j + 1) * news], uv[j]) for j in range(heads)]
-    out_d[...] = jnp.swapaxes(jnp.stack(done), 0, 1).astype(jnp.bfloat16).reshape(out_d.shape)
+    out_d[...] = jnp.swapaxes(jnp.stack(done_d), 0, 1).astype(jnp.bfloat16).reshape(out_d.shape)
 
 
 def body(
@@ -410,6 +431,7 @@
             pltpu.VMEM((n * chunk, lanes), jnp.float32),
             pltpu.VMEM((per_call * queries // lanes, n * chunk, lanes), jnp.float32),
             pltpu.VMEM((per_call * queries // lanes, n * chunk, lanes), bf),
+            pltpu.VMEM((news, (n + 1) * block), jnp.float32),
         ],
         compiler_params=pltpu.CompilerParams(vmem_limit_bytes=60 * 1024 * 1024),
         cost_estimate=pl.CostEstimate(

time: 57.6 us -> 56.9 us (0.988); the launches traced: 56.7 us -> 56.7 us
    pallas_call x1, Pallas kernels: 32.9 us -> 34.1 us  [body(): pl.pallas_call(functools.partial(gather, (n, nh, nz, ny, own, ppd, steps)...]
    pallas_call x1, Pallas kernels: 22.5 us -> 21.4 us  [body(): pl.pallas_call(functools.partial(attention, (n, nh, own, ppd, steps)), gr...]
where the time goes in v5:
time: 56.9 us; the launch traced here: 56.7 us
  Pallas kernels  55.4 us (97%)
  between operations  1.29 us (2%)
    pallas_call x1, Pallas kernels, body(): pl.pallas_call(functools.partial(gather, (n, nh, nz, ny, own, ppd, steps)...  34.1 us
    pallas_call x1, Pallas kernels, body(): pl.pallas_call(functools.partial(attention, (n, nh, own, ppd, steps)), gr...  21.4 us

profile of v5, /device:TPU:8, one launch (start us, length us, event | category | flops | bytes accessed | tf_op | source)
XLA Modules:
  0.0 56.7 jit_solution(351529578436684518)
XLA Ops:
  1.3 34.1 %shard_map.131 = (bf16[16,96,576]{2,1,0:T(8,128)(2,1)}, bf16[17,16,576]{2,1,0:T(8,128)(2,1)}, bf16[32,64,576]{2,1,0:T(8,128)(2,1)}, bf16[32,16,576]{2,1,0:T(8,128)(2,1)}) custom-call(bf16[96,576]{1,0:T(8,128)(2,1)} %prompt.1, bf16[64,32,192]{2,1,0:T(8,128)(2,1)} %query.1, bf16[4,4,32,192]{3,2,1,0:T(8,128)(2,1)} %dquery.1, bf16[32,128,512]{2,1,0:T(8,128)(2,1)} %w_uk.1, ...), custom_call_target="tpu_custom_call" | custom-call | flops 401604608 | bytes 9109504 | tf_op jit(solution)/shard_map/pallas_call | solution.py:369
  35.4 21.4 %shard_map.132 = (bf16[64,32,128]{2,1,0:T(8,128)(2,1)}, bf16[4,4,32,128]{3,2,1,0:T(8,128)(2,1)}) custom-call(s32[1]{0:T(128)S(6)} %copy.14.span, s32[4]{0:T(128)} %lengths.1, bf16[16,96,576]{2,1,0:T(8,128)(2,1)} %get-tuple-element.6.lat, bf16[17,16,576]{2,1,0:T(8,128)(2,1)} %get-tuple-element.7.keys, bf16[32,64,576]{2,1,0:T(8,128)(2,1)} %get-tuple-element.8.absp, ...), custom_call_target="tpu_custom_call" | custom-call | flops 6845104128 | bytes 8323072 | tf_op jit(solution)/shard_map/pallas_call | solution.py:412

commit v6 on v5

--- a/solution.py
+++ b/solution.py
@@ -189,20 +189,26 @@
         qt[:, pl.ds(at_q, 16), :] = jnp.swapaxes(qv[pl.ds(at_q, 16)], 0, 1)
         return 0
 
-    lax.fori_loop(0, queries // 16, turn, 0)
+    half = queries // 32
+    lax.fori_loop(0, half, turn, 0)
+    for dz in range(2, nz):
+        step(dz, 0)
+    lax.fori_loop(half, queries // 16, turn, 0)
     qt[:, queries:, :] = jnp.swapaxes(dqv[...].reshape(news, heads, dqv.shape[3]), 0, 1)
     loads[6].wait()
     loads[0].wait()
     pairs = heads // pair
-    per = -(-pairs // max(1, nz - 2))
-    for dz in range(2, nz):
-        step(dz, 0)
-        low, high = min(pairs, (dz - 2) * per), min(pairs, (dz - 1) * per)
+
+    def absorb_some(k, parts_of):
+        low, high = k * pairs // parts_of, (k + 1) * pairs // parts_of
         if high > low:
             lax.fori_loop(low, high, absorb, 0, unroll=4 if (high - low) % 4 == 0 else 1)
-    for dz in range(nz):
-        for dy in range(1, ny):
-            step(dz, dy)
+
+    far = [(dz, dy) for dz in range(nz) for dy in range(1, ny)]
+    for k, (dz, dy) in enumerate(far):
+        step(dz, dy)
+        if k < len(far) - 1:
+            absorb_some(k, len(far))
 
     for g in range(group):
         @pl.when(g * nh + hx != me)
@@ -222,6 +228,7 @@
     for k in range(1, nh):
         swap_copy(k, hx).start()
 
+    absorb_some(len(far) - 1, len(far))
     for k in range(1, nh):
         peer = lax.rem(hx + k, nh)
         pltpu.make_async_remote_copy(
@@ -301,10 +308,6 @@
         fits = jnp.where(place < n, jnp.where(cached_ok, 1, 0), jnp.where(new_ok, 1, 0))
         veto_d[...] = jnp.where((fits > 0) & (slot == rid % own), 0.0, LOW)
 
-    rows = 64
-    for g in range(heads // per_step):
-        q = absp[g * per_step : (g + 1) * per_step].reshape(lanes, width)
-        score[g] = nt_dot(lat[...].reshape(total, width), q)
     q = absd[...].reshape(heads * news, width)
     k = keys[...].reshape(kcount, width)
     s = (nt_dot(q, k).reshape(heads, news, kcount) + veto_d[...][None]).reshape(heads * news, kcount)
@@ -312,35 +315,51 @@
     p = jnp.exp2((s - m) * factor)
     norm = jnp.sum(p, axis=1, keepdims=True)
     mixed_d = (nn_dot(p.astype(jnp.bfloat16), k[:, :KV_RANK]) / norm).astype(jnp.bfloat16)
-    done, done_d = [], []
-    pair = 2 if per_step % 2 == 0 else 1
-    for g in range(heads // per_step):
-        top = jnp.full((8, lanes), LOW, jnp.float32)
-        for r in range(0, total, rows):
-            x = score[g, r : r + rows] + veto[r : r + rows]
-            score[g, r : r + rows] = x
-            top = jnp.maximum(top, jnp.max(x.reshape(rows // 8, 8, lanes), axis=0))
-        m = jnp.max(top, axis=0, keepdims=True)
-        norm = jnp.zeros((8, lanes), jnp.float32)
-        for r in range(0, total, rows):
-            p = jnp.exp2((score[g, r : r + rows] - m) * factor)
-            norm = norm + jnp.sum(p.reshape(rows // 8, 8, lanes), axis=0)
-            weight[g, r : r + rows] = p.astype(jnp.bfloat16)
-        norm = jnp.sum(norm, axis=0, keepdims=True)
-        mixed = (nn_dot(lat_t[...], weight[g]) / norm).T.astype(jnp.bfloat16)
-        for j in range(0, per_step, pair):
-            h = g * per_step + j
-            left = jnp.concatenate(
-                [mixed[j * queries : (j + pair) * queries], mixed_d[h * news : (h + pair) * news]], axis=0
-            )
-            o = nn_dot(left, jnp.concatenate([uv[h + k] for k in range(pair)], axis=1))
-            vdim = uv.shape[2]
-            for k in range(pair):
-                mine = o[:, k * vdim : (k + 1) * vdim]
-                done.append(mine[k * queries : (k + 1) * queries])
-                done_d.append(mine[pair * queries + k * news : pair * queries + (k + 1) * news])
-    out_p[...] = jnp.swapaxes(jnp.stack(done), 0, 1).astype(jnp.bfloat16)
-    out_d[...] = jnp.swapaxes(jnp.stack(done_d), 0, 1).astype(jnp.bfloat16).reshape(out_d.shape)
+    def run(depth):
+        rows = 64
+        for g in range(heads // per_step):
+            q = absp[g * per_step : (g + 1) * per_step].reshape(lanes, width)
+            score[g, :depth] = nt_dot(lat[...].reshape(total, width)[:depth], q)
+        done, done_d = [], []
+        pair = 2 if per_step % 2 == 0 else 1
+        for g in range(heads // per_step):
+            top = jnp.full((8, lanes), LOW, jnp.float32)
+            for r in range(0, depth, rows):
+                x = score[g, r : r + rows] + veto[r : r + rows]
+                score[g, r : r + rows] = x
+                top = jnp.maximum(top, jnp.max(x.reshape(rows // 8, 8, lanes), axis=0))
+            m = jnp.max(top, axis=0, keepdims=True)
+            norm = jnp.zeros((8, lanes), jnp.float32)
+            for r in range(0, depth, rows):
+                p = jnp.exp2((score[g, r : r + rows] - m) * factor)
+                norm = norm + jnp.sum(p.reshape(rows // 8, 8, lanes), axis=0)
+                weight[g, r : r + rows] = p.astype(jnp.bfloat16)
+            norm = jnp.sum(norm, axis=0, keepdims=True)
+            mixed = (nn_dot(lat_t[:, :depth], weight[g, :depth]) / norm).T.astype(jnp.bfloat16)
+            for j in range(0, per_step, pair):
+                h = g * per_step + j
+                left = jnp.concatenate(
+                    [mixed[j * queries : (j + pair) * queries], mixed_d[h * news : (h + pair) * news]], axis=0
+                )
+                o = nn_dot(left, jnp.concatenate([uv[h + k] for k in range(pair)], axis=1))
+                vdim = uv.shape[2]
+                for k in range(pair):
+                    mine = o[:, k * vdim : (k + 1) * vdim]
+                    done.append(mine[k * queries : (k + 1) * queries])
+                    done_d.append(mine[pair * queries + k * news : pair * queries + (k + 1) * news])
+        out_p[...] = jnp.swapaxes(jnp.stack(done), 0, 1).astype(jnp.bfloat16)
+        out_d[...] = jnp.swapaxes(jnp.stack(done_d), 0, 1).astype(jnp.bfloat16).reshape(out_d.shape)
+
+    short = total * 5 // 6 // 128 * 128
+    enough = first + queries <= short
+
+    @pl.when(enough)
+    def _():
+        run(short)
+
+    @pl.when(jnp.logical_not(enough))
+    def _():
+        run(total)
 
 
 def body(

time: 56.9 us -> 57 us (level); the launches traced: 56.7 us -> 56.1 us
  Pallas kernels: 55.4 us -> 54.8 us
    pallas_call x1, Pallas kernels: 21.4 us -> 20.8 us  [body(): pl.pallas_call(functools.partial(attention, (n, nh, own, ppd, steps)), gr...]
where the time goes in v6:
time: 57 us; the launch traced here: 56.1 us
  Pallas kernels  54.8 us (96%)
  between operations  1.29 us (2%)
    pallas_call x1, Pallas kernels, body(): pl.pallas_call(functools.partial(gather, (n, nh, nz, ny, own, ppd, steps)...  34.1 us
    pallas_call x1, Pallas kernels, body(): pl.pallas_call(functools.partial(attention, (n, nh, own, ppd, steps)), gr...  20.8 us

profile of v6, /device:TPU:8, one launch (start us, length us, event | category | flops | bytes accessed | tf_op | source)
XLA Modules:
  0.0 56.1 jit_solution(4313611233985690212)
XLA Ops:
  1.3 34.1 %shard_map.131 = (bf16[16,96,576]{2,1,0:T(8,128)(2,1)}, bf16[17,16,576]{2,1,0:T(8,128)(2,1)}, bf16[32,64,576]{2,1,0:T(8,128)(2,1)}, bf16[32,16,576]{2,1,0:T(8,128)(2,1)}) custom-call(bf16[96,576]{1,0:T(8,128)(2,1)} %prompt.1, bf16[64,32,192]{2,1,0:T(8,128)(2,1)} %query.1, bf16[4,4,32,192]{3,2,1,0:T(8,128)(2,1)} %dquery.1, bf16[32,128,512]{2,1,0:T(8,128)(2,1)} %w_uk.1, ...), custom_call_target="tpu_custom_call" | custom-call | flops 401604608 | bytes 9109504 | tf_op jit(solution)/shard_map/pallas_call | solution.py:388
  35.4 20.8 %shard_map.132 = (bf16[64,32,128]{2,1,0:T(8,128)(2,1)}, bf16[4,4,32,128]{3,2,1,0:T(8,128)(2,1)}) custom-call(s32[1]{0:T(128)S(6)} %copy.14.span, s32[4]{0:T(128)} %lengths.1, bf16[16,96,576]{2,1,0:T(8,128)(2,1)} %get-tuple-element.6.lat, bf16[17,16,576]{2,1,0:T(8,128)(2,1)} %get-tuple-element.7.keys, bf16[32,64,576]{2,1,0:T(8,128)(2,1)} %get-tuple-element.8.absp, ...), custom_call_target="tpu_custom_call" | custom-call | flops 6845104128 | bytes 8323072 | tf_op jit(solution)/shard_map/pallas_call | solution.py:431
